TPU v7x, 32 devices: a whole 2x2x4 slice. The times are simulated.
32 devices in a mesh: row: 4 (over y, x), col: 8 (over z, core).
Axes of the slice: x: 2, y: 2, z: 4, core: 2. Of those that a mesh axis runs over, the one named last changes fastest.
Arguments:
- features: bfloat16 [16384, 256], P(('col', 'row')), may hold values from -6 to 6
- weight: bfloat16 [256, 256], replicated, may hold values from -0.375 to 0.375
- bias: float32 [256], replicated, may hold values from -4 to 4
- cotangent: bfloat16 [16384, 256], P(('row', 'col')), may hold values from -6 to 6
- tiles: bfloat16 [4, 8, 384, 128, 128], P('row', 'col'), may hold values from -0.0546875 to 0.0546875
- tile_rows: int32 [4, 8, 384], P('row', 'col'), may hold values from 0 to 31, as said below
- tile_cols: int32 [4, 8, 384], P('row', 'col'), may hold values from 0 to 15
- tile_counts: int32 [4, 8], P('row', 'col'), may hold values from 24 to 384, as said below
Outputs:
- hidden: bfloat16 [16384, 256], P(('row', 'col'))
- grad_weight: float32 [256, 256], replicated
- grad_bias: float32 [256], replicated
- grad_features: bfloat16 [16384, 256], P(('col', 'row'))
Inputs may be any that keep to these rules, and one draw needn't show every extreme that they name: `tile_rows`: on each grid cell the slots name distinct blocks. `tile_counts`: slots at or after a cell's count are unused; some cell uses all 384 slots.
All inputs are finite; a program needn't handle non-finite values.
Results may differ from a plain program's by a relative error of at most 0.013.
Values may be sent and summed in bfloat16 or wider, within the bound.
No kernel may reach another device: no remote copies, remote signals or barrier semaphores. Data moves between devices by JAX's collectives and lax.ppermute only.
A program may use at most 128 MiB of HBM per device.

v0:
```python
import math

import jax
import jax.numpy as jnp
from jax import lax
from jax.experimental import pallas as pl
from jax.experimental.pallas import tpu as pltpu
from jax.sharding import PartitionSpec as P

BF16 = jnp.bfloat16
F32 = jnp.float32
CELL_IN_VMEM = 1 << 24


def densify_kernel(per, half, one_band, rows_ref, cols_ref, count_ref, *refs):
    *window_refs, cell_ref = refs
    group, block, _ = window_refs[0].shape
    band = pl.program_id(0)
    step = pl.program_id(1)
    row_pos = lax.axis_index("row")
    col_pos = lax.axis_index("col")

    @pl.when(step == 0)
    def _():
        def clear(index, carry):
            cell_ref[pl.ds(pl.multiple_of(index * block, block), block), :] = jnp.zeros(
                (block, cell_ref.shape[1]), cell_ref.dtype
            )
            return carry

        lax.fori_loop(0, cell_ref.shape[0] // block, clear, 0)

    def put(window_ref, start, first, number):
        places = []
        for index in range(number):
            row = rows_ref[0, 0, start + first + index]
            col = cols_ref[0, 0, start + first + index]
            panel = lax.div(row, per)
            down = panel ^ col_pos
            down = (down & 1) * half + (down >> 1)
            top = ((down - panel) * per + row) * block - band * cell_ref.shape[0]
            panel = lax.div(col, per)
            left = (((panel ^ row_pos) - panel) * per + col) * block
            places.append((top, left))
        values = [window_ref[first + index] for index in range(number)]
        for (top, left), value in zip(places, values):

            def store(top=top, left=left, value=value):
                cell_ref[
                    pl.ds(pl.multiple_of(top, block), block),
                    pl.ds(pl.multiple_of(left, block), block),
                ] = value

            if one_band:
                store()
            else:
                pl.when((top >= 0) & (top < cell_ref.shape[0]))(store)

    for part, window_ref in enumerate(window_refs):
        start = (step * len(window_refs) + part) * group
        live = jnp.clip(count_ref[0, 0] - start, 0, group)

        def put_four(index, carry, window_ref=window_ref, start=start):
            put(window_ref, start, index * 4, 4)
            return carry

        lax.fori_loop(0, live >> 2, put_four, 0)

        def put_one(index, carry, window_ref=window_ref, start=start):
            put(window_ref, start, index, 1)
            return carry

        lax.fori_loop((live >> 2) << 2, live, put_one, 0)


def densify(tiles, rows, cols, count, per, col_count, row_count):
    slots, block, _ = tiles.shape
    group = math.gcd(slots, 32)
    windows = math.gcd(slots // group, 3)
    shape = (per * col_count * block, per * row_count * block)
    size = shape[0] * shape[1] * 2
    bands = max(1, size // CELL_IN_VMEM)
    space = pltpu.VMEM if bands == 1 else pltpu.HBM

    def tile_spec(part):
        def tile_map(band, step, rows_ref, cols_ref, count_ref):
            last = jnp.maximum(count_ref[0, 0] - 1, 0) // group
            return (jnp.minimum(step * windows + part, last), 0, 0)

        return pl.BlockSpec((group, block, block), tile_map)

    tiles = pltpu.with_memory_space_constraint(tiles, pltpu.HBM)
    return pl.pallas_call(
        lambda *refs: densify_kernel(per, col_count // 2, bands == 1, *refs),
        out_shape=space(shape, tiles.dtype),
        grid_spec=pltpu.PrefetchScalarGridSpec(
            num_scalar_prefetch=3,
            grid=(bands, slots // (group * windows)),
            in_specs=[tile_spec(part) for part in range(windows)],
            out_specs=pl.BlockSpec(
                (shape[0] // bands, shape[1]),
                lambda band, step, *refs: (band, 0),
                pipeline_mode=pl.Buffered(1),
            ),
        ),
        compiler_params=pltpu.CompilerParams(
            vmem_limit_bytes=size // bands + (10 << 20)
        ),
        cost_estimate=pl.CostEstimate(
            flops=0, bytes_accessed=2 * size, transcendentals=0
        ),
        name="densify",
    )(
        pltpu.with_memory_space_constraint(rows, pltpu.HBM),
        pltpu.with_memory_space_constraint(cols, pltpu.HBM),
        count,
        *[tiles] * windows,
    )


def dense_kernel(part_count, *refs):
    own_ref = refs[0]
    part_refs = refs[1 : 1 + part_count]
    weight_ref, bias_ref, cotangent_ref = refs[1 + part_count : 4 + part_count]
    hidden_ref, grad_ref, local_ref = refs[4 + part_count :]
    total = own_ref[...]
    for part_ref in part_refs:
        total = total + part_ref[...].astype(F32)
    aggregated = total.astype(BF16)
    weight = weight_ref[...]
    preact = jnp.dot(aggregated, weight, preferred_element_type=F32) + bias_ref[...]
    sigma = jax.nn.sigmoid(preact)
    hidden_ref[...] = (preact * sigma).astype(BF16)
    slope = sigma * (1.0 + preact * (1.0 - sigma))
    grad_pre = (cotangent_ref[...].astype(F32) * slope).astype(BF16)
    grad_ref[...] = lax.dot_general(
        weight, grad_pre, (((1,), (1,)), ((), ())), preferred_element_type=F32
    ).astype(BF16)
    width = weight.shape[0]
    local_ref[:width] = lax.dot_general(
        aggregated, grad_pre, (((0,), (0,)), ((), ())), preferred_element_type=F32
    )
    local_ref[width:] = jnp.broadcast_to(
        jnp.sum(grad_pre.astype(F32), axis=0, keepdims=True),
        (local_ref.shape[0] - width, width),
    )


def dense(own, parts, weight, bias, cotangent):
    nodes, width = own.shape
    spec = pl.BlockSpec(memory_space=pltpu.VMEM)
    shapes = (
        jax.ShapeDtypeStruct((nodes, width), BF16),
        jax.ShapeDtypeStruct((width, nodes), BF16),
        jax.ShapeDtypeStruct((width + 16, width), F32),
    )
    return pl.pallas_call(
        lambda *refs: dense_kernel(len(parts), *refs),
        out_shape=shapes,
        in_specs=[spec] * (4 + len(parts)),
        out_specs=(spec,) * 3,
        compiler_params=pltpu.CompilerParams(vmem_limit_bytes=16 << 20),
        cost_estimate=pl.CostEstimate(
            flops=6 * nodes * width * width,
            bytes_accessed=8 * nodes * width,
            transcendentals=nodes * width,
        ),
        name="dense",
    )(own, *parts, weight, bias.reshape(1, width), cotangent)


def back_kernel(panels, chosen, last, with_total, *refs):
    cell_ref, *grad_refs = refs[: 1 + len(panels)]
    rest = refs[1 + len(panels) :]
    width, nodes = grad_refs[0].shape
    runs = []
    for panel, ref in zip(panels, grad_refs):
        if runs and runs[-1][0] + len(runs[-1][1]) == panel:
            runs[-1][1].append(ref[...])
        else:
            runs.append((panel, [ref[...]]))
    runs = [(panel * nodes, jnp.concatenate(grads, axis=1)) for panel, grads in runs]

    def product(columns):
        value = None
        for top, grads in runs:
            part = jnp.dot(
                grads,
                cell_ref[top : top + grads.shape[1], columns],
                preferred_element_type=F32,
            )
            value = part if value is None else value + part
        return value

    out_refs = rest[with_total:]
    for index, panel in enumerate(chosen):
        columns = slice(panel * nodes, (panel + 1) * nodes)
        value = product(columns)
        if with_total:
            value = rest[0][:, columns] + value
        if last:
            out_refs[index][...] = value.T.astype(out_refs[index].dtype)
        else:
            out_refs[0][:, columns] = value


def back(panels, chosen, grads, cell, total=None, last=False):
    width, nodes = grads[0].shape
    spec = pl.BlockSpec(memory_space=pltpu.VMEM)
    operands = (cell, *grads) if total is None else (cell, *grads, total)
    if not last:
        outs = (pltpu.VMEM((width, cell.shape[1]), F32),)
    else:
        outs = tuple(
            pltpu.VMEM((nodes, width), F32 if panel == 0 else BF16) for panel in chosen
        )
    flops = 2 * len(panels) * len(chosen) * nodes * nodes * width
    return pl.pallas_call(
        lambda *refs: back_kernel(panels, chosen, last, total is not None, *refs),
        out_shape=outs,
        in_specs=[spec] * len(operands),
        out_specs=[spec] * len(outs),
        compiler_params=pltpu.CompilerParams(vmem_limit_bytes=24 << 20),
        cost_estimate=pl.CostEstimate(
            flops=flops, bytes_accessed=flops // 512, transcendentals=0
        ),
        name="back_last" if last else "back",
    )(*operands)


def finish_kernel(factor, value_ref, part_ref, other_ref, out_ref, weight_ref, bias_ref):
    out_ref[...] = value_ref[...].astype(out_ref.dtype)
    summed = (part_ref[...].astype(F32) + other_ref[...].astype(F32)) * factor
    width = weight_ref.shape[0]
    weight_ref[...] = summed[:width]
    bias_ref[...] = summed[width : width + 1]


def finish(value, part, other, factor):
    spec = pl.BlockSpec(memory_space=pltpu.VMEM)
    nodes, width = value.shape
    return pl.pallas_call(
        lambda *refs: finish_kernel(factor, *refs),
        out_shape=(
            jax.ShapeDtypeStruct((nodes, width), BF16),
            jax.ShapeDtypeStruct((width, width), F32),
            jax.ShapeDtypeStruct((1, width), F32),
        ),
        in_specs=[spec] * 3,
        out_specs=(spec,) * 3,
        compiler_params=pltpu.CompilerParams(vmem_limit_bytes=16 << 20),
        cost_estimate=pl.CostEstimate(
            flops=8 * nodes * width, bytes_accessed=16 * nodes * width, transcendentals=0
        ),
        name="finish",
    )(value, part, other)


def swap(value, axis, mask):
    count = lax.axis_size(axis)
    return lax.ppermute(value, axis, [(i, i ^ mask) for i in range(count)])


def move(value, pairs):
    pairs = [(2 * a + core, 2 * b + core) for a, b in pairs for core in range(2)]
    return lax.ppermute(value, "col", pairs)


def sum_far(far, chunk, ready):
    if lax.axis_size("col") != 8:
        count = lax.axis_size("col") // 2
        parts = [swap(chunk(k, far).astype(BF16), "col", 2 * k) for k in range(1, count - 1)]
        return [*parts, swap(far, "col", 2 * (count - 1))], chunk(0, far)
    passed = jnp.where(at_end(), 0.0, swap(far, "col", 2).astype(F32))
    later, ready = lax.optimization_barrier((far, ready))
    middle = move(later, [(1, 2), (2, 1)])
    both = (chunk(2, passed) + passed).astype(BF16)
    across = swap(both, "col", 4)
    near = swap(chunk(1, both).astype(BF16), "col", 2)
    return [near, across, middle], chunk(0, both)


def gather_far(value, count):
    if count != 4:
        return [value] + [swap(value, "col", 2 * k) for k in range(1, count)]
    across = swap(value, "col", 4)
    near = swap(value, "col", 2)
    passed = swap(across, "col", 2)
    middle = move(value, [(1, 2), (2, 1)])
    return [value, near, across, jnp.where(at_end(), passed, middle)]


def at_end():
    place = lax.axis_index("col") // 2
    return (place == 0) | (place == lax.axis_size("col") // 2 - 1)


def sum_over(value, axis, masks):
    for mask in masks:
        value = value.astype(BF16)
        value = value.astype(F32) + swap(value, axis, mask).astype(F32)
    return value


def doublings(first, end):
    return [first << power for power in range((end // first).bit_length() - 1)]


def per_device(features, weight, bias, cotangent, tiles, tile_rows, tile_cols, tile_counts):
    block = tiles.shape[-1]
    nodes, width = features.shape
    row_count = lax.axis_size("row")
    col_count = lax.axis_size("col")
    half = col_count // 2
    factor = 1.0 / math.sqrt(nodes * row_count * col_count)

    source = jnp.zeros((row_count * nodes, width), BF16).at[:nodes].set(features)
    for k in range(row_count - 1, 0, -1):
        source = source.at[k * nodes : (k + 1) * nodes].set(swap(features, "row", k))
    cell = densify(
        tiles[0, 0], tile_rows, tile_cols, tile_counts, nodes // block, col_count, row_count
    )

    def cell_rows(core, k):
        top = (core * half + k) * nodes
        return cell[top : top + nodes]


    def cell_product(core, k, source):
        return jnp.dot(cell_rows(core, k), source, preferred_element_type=F32)

    far = half - 1
    from_mate = {
        k: swap(cell_product(1, k, source).astype(BF16), "col", 1) for k in (far, far - 1)
    }
    own_far = lax.optimization_barrier(cell_product(0, far, source))
    own_far = (own_far + from_mate[far].astype(F32)).astype(BF16)

    later, from_mate[far - 1] = lax.optimization_barrier((source, from_mate[far - 1]))
    for k in range(far - 1):
        from_mate[k] = swap(cell_product(1, k, later).astype(BF16), "col", 1)

    def chunk(k, hold):
        after, hold = lax.optimization_barrier((source, hold))
        return cell_product(0, k, after) + from_mate[k].astype(F32)

    parts, own = sum_far(own_far, chunk, from_mate[far - 1])
    hidden, grad_agg, local = dense(own, parts, weight, bias, cotangent)

    part = local + swap(local, "col", 1)
    part = sum_over(part, "row", doublings(1, row_count)).astype(BF16)
    own_grads = gather_far(grad_agg, half)
    mate_grads = [swap(grads, "col", 1) for grads in own_grads[:far]]

    if cell.size * 2 <= CELL_IN_VMEM:
        every = list(range(row_count))
        (total,) = back(list(range(far)), every, own_grads[:far], cell)
        (total,) = back(list(range(half, half + far)), every, mate_grads, cell, total)
        panels = [far, half + far]
        grads = [own_grads[far], swap(own_grads[far], "col", 1)]
        pieces = {}
        rest = total
        for chosen in ([row_count - 1], list(range(row_count - 2, 0, -1)), [0]):
            pieces.update(zip(chosen, back(panels, chosen, grads, cell, rest, True)))
            rest, pieces[chosen[-1]] = lax.optimization_barrier((total, pieces[chosen[-1]]))
    else:
        own = jnp.concatenate(own_grads, axis=1)
        mate_grads.append(swap(own_grads[far], "col", 1))
        mate = jnp.concatenate(mate_grads, axis=1)
        total = jnp.dot(own, cell[: half * nodes], preferred_element_type=F32)
        total = total + jnp.dot(mate, cell[half * nodes :], preferred_element_type=F32)
        pieces = {
            k: total[:, k * nodes : (k + 1) * nodes].T.astype(F32 if k == 0 else BF16)
            for k in range(row_count)
        }
    part, pieces[1] = lax.optimization_barrier((part, pieces[1]))
    landed = [swap(pieces[k], "row", k) for k in range(row_count - 1, 0, -1)]
    *masks, mask = doublings(2, col_count)
    part = sum_over(part, "col", masks).astype(BF16)
    value = pieces[0]
    for piece in landed:
        value = value + piece.astype(F32)
    grad_features, grad_weight, grad_bias = finish(value, part, swap(part, "col", mask), factor)
    return (hidden, grad_weight, grad_bias[0], grad_features)


def solution(mesh):
    in_specs = (
        P(("col", "row"), None),
        P(),
        P(),
        P(("row", "col"), None),
        P("row", "col", None, None, None),
        P("row", "col", None),
        P("row", "col", None),
        P("row", "col"),
    )
    out_specs = (P(("row", "col"), None), P(), P(), P(("col", "row"), None))
    return jax.shard_map(
        per_device, mesh=mesh, in_specs=in_specs, out_specs=out_specs, check_vma=False
    )
```

profile of v0, /device:TPU:0, one launch (start us, length us, event | category | flops | bytes accessed | tf_op | source)
XLA Modules:
  0.0 94.5 jit_solution(16230808538494917513)
XLA Ops:
  0.6 4.0 %collective-permute-start = (bf16[512,256]{1,0:T(8,128)(2,1)}, bf16[512,256]{1,0:T(8,128)(2,1)S(1)}, u32[]{:S(2)}, u32[]{:S(2)}) collective-permute-start(bf16[512,256]{1,0:T(8,128)(2,1)} %param.16), channel_id=1, source_target_pairs={{0,24},{8,16},{16,8},{24,0},{1,25},{9,17},{17,9},{25,1},{2,26},{10... | collective-permute-start | bytes 786440 | tf_op jit(solution)/shard_map/ppermute | solution.py:261
  4.6 0.5 collective-permute-start.1
  5.9 1.0 %scatter.14 = bf16[2048,256]{1,0:T(8,128)(2,1)S(1)} pad(bf16[512,256]{1,0:T(8,128)(2,1)} %param.16, bf16[]{:T(256)} %constant.127.clone.1), padding=0_1536x0_0 | pad | bytes 1310722 | tf_op jit(solution)/shard_map/scatter | solution.py:317
  6.9 6.4 %densify.1.refs_0_ = bf16[4096,2048]{1,0:T(8,128)(2,1)S(1)} custom-call(s32[1,1,384]{2,1,0:T(1,128)} %refs_0_.1, s32[1,1,384]{2,1,0:T(1,128)} %refs_1_.1, s32[1,1]{1,0:T(1,128)S(6)} %copy.15.refs_2_, bf16[384,128,128]{2,1,0:T(8,128)(2,1)} %bitcast.12, bf16[384,128,128]{2,1,0:T(8,128)(2,1)} %bitcast.13, bf16[384,128,128]{2,1,0:T(8,128)(2,1)} %bitcast.14), custom_call_target="tpu_custom_call" | custom-call | bytes 33554432 | tf_op jit(solution)/shard_map/densify/pallas_call | solution.py:93
  13.4 3.3 %collective-permute-done.1 = bf16[512,256]{1,0:T(8,128)(2,1)S(1)} collective-permute-done((bf16[512,256]{1,0:T(8,128)(2,1)}, bf16[512,256]{1,0:T(8,128)(2,1)S(1)}, u32[]{:S(2)}, u32[]{:S(2)}) %collective-permute-start.1) | collective-permute-done | bytes 262176 | tf_op jit(solution)/shard_map/ppermute | solution.py:261
  16.7 0.3 collective-permute-done.2
  17.0 0.7 fusion.37
  17.8 0.7 fusion.34
  18.5 0.5 collective-permute-start.5
  19.0 0.7 fusion.10
  19.8 0.7 collective-permute-done.5
  20.4 0.7 fusion.40
  21.2 0.2 collective-permute-start.6
  21.5 1.7 %collective-permute-start.4 = (bf16[512,256]{1,0:T(8,128)(2,1)S(1)}, bf16[512,256]{1,0:T(8,128)(2,1)S(1)}, u32[]{:S(2)}, u32[]{:S(2)}) collective-permute-start(bf16[512,256]{1,0:T(8,128)(2,1)S(1)} %add_convert_fusion), channel_id=1, source_target_pairs={{0,2},{1,3},{2,0},{3,1},{4,6},{5,7},{6,4},{7,5},{8,10},{9,11},{10,... | collective-permute-start | bytes 786440 | tf_op jit(solution)/shard_map/ppermute | solution.py:261
  23.1 0.7 fusion.43
  23.8 0.1 collective-permute-start.7
  24.0 0.7 collective-permute-start.10
  24.6 5.5 %collective-permute-done.4 = bf16[512,256]{1,0:T(8,128)(2,1)S(1)} collective-permute-done((bf16[512,256]{1,0:T(8,128)(2,1)S(1)}, bf16[512,256]{1,0:T(8,128)(2,1)S(1)}, u32[]{:S(2)}, u32[]{:S(2)}) %collective-permute-start.4) | collective-permute-done | bytes 262176 | tf_op jit(solution)/shard_map/ppermute | solution.py:261
  30.1 0.7 fusion.31
  30.8 3.1 %collective-permute-start.9 = (bf16[512,256]{1,0:T(8,128)(2,1)S(1)}, bf16[512,256]{1,0:T(8,128)(2,1)S(1)}, u32[]{:S(2)}, u32[]{:S(2)}) collective-permute-start(bf16[512,256]{1,0:T(8,128)(2,1)S(1)} %fusion.31), channel_id=1, source_target_pairs={{0,4},{1,5},{2,6},{3,7},{4,0},{5,1},{6,2},{7,3},{8,12},{9,13},{10,... | collective-permute-start | bytes 786440 | tf_op jit(solution)/shard_map/ppermute | solution.py:261
  33.9 0.7 fusion.28
  34.6 1.6 %collective-permute-start.8 = (bf16[512,256]{1,0:T(8,128)(2,1)S(1)}, bf16[512,256]{1,0:T(8,128)(2,1)S(1)}, u32[]{:S(2)}, u32[]{:S(2)}) collective-permute-start(bf16[512,256]{1,0:T(8,128)(2,1)S(1)} %fusion.28), channel_id=1, source_target_pairs={{0,2},{1,3},{2,0},{3,1},{4,6},{5,7},{6,4},{7,5},{8,10},{9,11},{10,... | collective-permute-start | bytes 786440 | tf_op jit(solution)/shard_map/ppermute | solution.py:261
  36.3 0.7 fusion.16.refs_0_
  37.0 10.8 %collective-permute-done.8.refs_1_ = bf16[512,256]{1,0:T(8,128)(2,1)S(1)} collective-permute-done((bf16[512,256]{1,0:T(8,128)(2,1)S(1)}, bf16[512,256]{1,0:T(8,128)(2,1)S(1)}, u32[]{:S(2)}, u32[]{:S(2)}) %collective-permute-start.8) | collective-permute-done | bytes 262176 | tf_op jit(solution)/shard_map/ppermute | solution.py:261
  47.8 1.1 %dense.1 = (bf16[512,256]{1,0:T(8,128)(2,1)}, bf16[256,512]{1,0:T(8,128)(2,1)S(1)}, f32[272,256]{1,0:T(8,128)S(1)}) custom-call(f32[512,256]{1,0:T(8,128)S(1)} %fusion.16.refs_0_, bf16[512,256]{1,0:T(8,128)(2,1)S(1)} %collective-permute-done.8.refs_1_, bf16[512,256]{1,0:T(8,128)(2,1)S(1)} %collective-permute-done.9.refs_2_, ...), custom_call_target="tpu_custom_call" | custom-call | flops 201326592 | bytes 1048576 | tf_op jit(solution)/shard_map/dense/pallas_call | solution.py:157
  48.9 2.4 %collective-permute-start.12 = (bf16[256,512]{1,0:T(8,128)(2,1)S(1)}, bf16[256,512]{1,0:T(8,128)(2,1)S(1)}, u32[]{:S(2)}, u32[]{:S(2)}) collective-permute-start(bf16[256,512]{1,0:T(8,128)(2,1)S(1)} %get-tuple-element.78.refs_1_), channel_id=1, source_target_pairs={{0,2},{1,3},{2,0},{3,1},{4,6},{5,7},{6,4},{7,5},{8,10},{9,11},{10,... | collective-permute-start | bytes 786440 | tf_op jit(solution)/shard_map/ppermute | solution.py:261
  51.3 0.8 collective-permute-start.17
  52.3 11.2 %collective-permute-done.14.refs_3_ = bf16[256,512]{1,0:T(8,128)(2,1)S(1)} collective-permute-done((bf16[256,512]{1,0:T(8,128)(2,1)S(1)}, bf16[256,512]{1,0:T(8,128)(2,1)S(1)}, u32[]{:S(2)}, u32[]{:S(2)}) %collective-permute-start.14) | collective-permute-done | bytes 262176 | tf_op jit(solution)/shard_map/ppermute | solution.py:261
  63.7 1.1 %collective-permute-start.22 = (bf16[272,256]{1,0:T(8,128)(2,1)S(1)}, bf16[272,256]{1,0:T(8,128)(2,1)S(1)}, u32[]{:S(2)}, u32[]{:S(2)}) collective-permute-start(bf16[272,256]{1,0:T(8,128)(2,1)S(1)} %add_convert_fusion.4), channel_id=1, source_target_pairs={{0,8},{8,0},{16,24},{24,16},{1,9},{9,1},{17,25},{25,17},{2,10},{10... | collective-permute-start | bytes 417800 | tf_op jit(solution)/shard_map/ppermute | solution.py:261
  64.7 1.8 %back.2.refs_4_ = f32[256,2048]{1,0:T(8,128)S(1)} custom-call(bf16[4096,2048]{1,0:T(8,128)(2,1)S(1)} %densify.1.refs_0_, bf16[256,512]{1,0:T(8,128)(2,1)S(1)} %get-tuple-element.78.refs_1_, bf16[256,512]{1,0:T(8,128)(2,1)S(1)} %collective-permute-done.12.refs_2_, bf16[256,512]{1,0:T(8,128)(2,1)S(1)} %collective-permute-done.14.refs_3_), custom_call_target="tpu_custom_call" | custom-call | flops 1610612736 | bytes 3145728 | tf_op jit(solution)/shard_map/back/pallas_call | solution.py:218
  66.5 3.2 %collective-permute-done.22 = bf16[272,256]{1,0:T(8,128)(2,1)S(1)} collective-permute-done((bf16[272,256]{1,0:T(8,128)(2,1)S(1)}, bf16[272,256]{1,0:T(8,128)(2,1)S(1)}, u32[]{:S(2)}, u32[]{:S(2)}) %collective-permute-start.22) | collective-permute-done | bytes 139296 | tf_op jit(solution)/shard_map/ppermute | solution.py:261
  69.8 1.1 %collective-permute-start.23 = (bf16[272,256]{1,0:T(8,128)(2,1)S(1)}, bf16[272,256]{1,0:T(8,128)(2,1)S(1)}, u32[]{:S(2)}, u32[]{:S(2)}) collective-permute-start(bf16[272,256]{1,0:T(8,128)(2,1)S(1)} %add_convert_fusion.3), channel_id=1, source_target_pairs={{0,16},{8,24},{16,0},{24,8},{1,17},{9,25},{17,1},{25,9},{2,18},{10... | collective-permute-start | bytes 417800 | tf_op jit(solution)/shard_map/ppermute | solution.py:261
  70.8 0.9 collective-permute-done.16
  71.9 1.8 %back.3.refs_3_ = f32[256,2048]{1,0:T(8,128)S(1)} custom-call(bf16[4096,2048]{1,0:T(8,128)(2,1)S(1)} %densify.1.refs_0_, bf16[256,512]{1,0:T(8,128)(2,1)S(1)} %collective-permute-done.11.refs_1_, bf16[256,512]{1,0:T(8,128)(2,1)S(1)} %collective-permute-done.13.refs_2_, bf16[256,512]{1,0:T(8,128)(2,1)S(1)} %collective-permute-done.15.refs_3_, ...), custom_call_target="tpu_custom_call" | custom-call | flops 1610612736 | bytes 3145728 | tf_op jit(solution)/shard_map/back/pallas_call | solution.py:218
  73.7 2.3 %collective-permute-done.23 = bf16[272,256]{1,0:T(8,128)(2,1)S(1)} collective-permute-done((bf16[272,256]{1,0:T(8,128)(2,1)S(1)}, bf16[272,256]{1,0:T(8,128)(2,1)S(1)}, u32[]{:S(2)}, u32[]{:S(2)}) %collective-permute-start.23) | collective-permute-done | bytes 139296 | tf_op jit(solution)/shard_map/ppermute | solution.py:261
  76.0 0.5 back_last.3
  76.5 0.8 back_last.4
  77.3 2.1 %collective-permute-start.25 = (bf16[272,256]{1,0:T(8,128)(2,1)S(1)}, bf16[272,256]{1,0:T(8,128)(2,1)S(1)}, u32[]{:S(2)}, u32[]{:S(2)}) collective-permute-start(bf16[272,256]{1,0:T(8,128)(2,1)S(1)} %add_convert_fusion.2), channel_id=1, source_target_pairs={{0,2},{1,3},{2,0},{3,1},{4,6},{5,7},{6,4},{7,5},{8,10},{9,11},{10,... | collective-permute-start | bytes 417800 | tf_op jit(solution)/shard_map/ppermute | solution.py:261
  79.3 1.2 %collective-permute-start.19 = (bf16[512,256]{1,0:T(8,128)(2,1)S(1)}, bf16[512,256]{1,0:T(8,128)(2,1)S(1)}, u32[]{:S(2)}, u32[]{:S(2)}) collective-permute-start(bf16[512,256]{1,0:T(8,128)(2,1)S(1)} %back_last.3), channel_id=1, source_target_pairs={{0,24},{8,16},{16,8},{24,0},{1,25},{9,17},{17,9},{25,1},{2,26},{10... | collective-permute-start | bytes 786440 | tf_op jit(solution)/shard_map/ppermute | solution.py:261
  80.6 1.2 %collective-permute-start.24 = (bf16[512,256]{1,0:T(8,128)(2,1)S(1)}, bf16[512,256]{1,0:T(8,128)(2,1)S(1)}, u32[]{:S(2)}, u32[]{:S(2)}) collective-permute-start(bf16[512,256]{1,0:T(8,128)(2,1)S(1)} %get-tuple-element.87), channel_id=1, source_target_pairs={{0,8},{8,0},{16,24},{24,16},{1,9},{9,1},{17,25},{25,17},{2,10},{10... | collective-permute-start | bytes 786440 | tf_op jit(solution)/shard_map/ppermute | solution.py:261
  81.8 1.0 %collective-permute-start.20 = (bf16[512,256]{1,0:T(8,128)(2,1)S(1)}, bf16[512,256]{1,0:T(8,128)(2,1)S(1)}, u32[]{:S(2)}, u32[]{:S(2)}) collective-permute-start(bf16[512,256]{1,0:T(8,128)(2,1)S(1)} %get-tuple-element.84), channel_id=1, source_target_pairs={{0,16},{8,24},{16,0},{24,8},{1,17},{9,25},{17,1},{25,9},{2,18},{10... | collective-permute-start | bytes 786440 | tf_op jit(solution)/shard_map/ppermute | solution.py:261
  82.8 0.6 back_last.5
  83.5 1.8 %collective-permute-start.26 = (bf16[272,256]{1,0:T(8,128)(2,1)S(1)}, bf16[272,256]{1,0:T(8,128)(2,1)S(1)}, u32[]{:S(2)}, u32[]{:S(2)}) collective-permute-start(bf16[272,256]{1,0:T(8,128)(2,1)S(1)} %add_convert_fusion.1.refs_1_), channel_id=1, source_target_pairs={{0,4},{1,5},{2,6},{3,7},{4,0},{5,1},{6,2},{7,3},{8,12},{9,13},{10,... | collective-permute-start | bytes 417800 | tf_op jit(solution)/shard_map/ppermute | solution.py:261
  85.3 4.3 %collective-permute-done.19 = bf16[512,256]{1,0:T(8,128)(2,1)S(1)} collective-permute-done((bf16[512,256]{1,0:T(8,128)(2,1)S(1)}, bf16[512,256]{1,0:T(8,128)(2,1)S(1)}, u32[]{:S(2)}, u32[]{:S(2)}) %collective-permute-start.19) | collective-permute-done | bytes 262176 | tf_op jit(solution)/shard_map/ppermute | solution.py:261
  89.5 3.6 %collective-permute-done.24 = bf16[512,256]{1,0:T(8,128)(2,1)S(1)} collective-permute-done((bf16[512,256]{1,0:T(8,128)(2,1)S(1)}, bf16[512,256]{1,0:T(8,128)(2,1)S(1)}, u32[]{:S(2)}, u32[]{:S(2)}) %collective-permute-start.24) | collective-permute-done | bytes 262176 | tf_op jit(solution)/shard_map/ppermute | solution.py:261
  93.1 0.4 collective-permute-done.20
  93.5 0.1 convert_add_fusion.refs_0_
  93.7 0.8 finish.1
  (39 shorter events, 0.8 us)
Async XLA Ops:
  0.6 12.7 %collective-permute-start = (bf16[512,256]{1,0:T(8,128)(2,1)}, bf16[512,256]{1,0:T(8,128)(2,1)S(1)}, u32[]{:S(2)}, u32[]{:S(2)}) collective-permute-start(bf16[512,256]{1,0:T(8,128)(2,1)} %param.16), channel_id=1, source_target_pairs={{0,24},{8,16},{16,8},{24,0},{1,25},{9,17},{17,9},{25,1},{2,26},{10... | collective-permute-start | bytes 786440 | tf_op jit(solution)/shard_map/ppermute | solution.py:261
  4.6 12.1 %collective-permute-start.1 = (bf16[512,256]{1,0:T(8,128)(2,1)}, bf16[512,256]{1,0:T(8,128)(2,1)S(1)}, u32[]{:S(2)}, u32[]{:S(2)}) collective-permute-start(bf16[512,256]{1,0:T(8,128)(2,1)} %param.16), channel_id=1, source_target_pairs={{0,16},{8,24},{16,0},{24,8},{1,17},{9,25},{17,1},{25,9},{2,18},{10... | collective-permute-start | bytes 786440 | tf_op jit(solution)/shard_map/ppermute | solution.py:261
  5.1 11.9 %collective-permute-start.2 = (bf16[512,256]{1,0:T(8,128)(2,1)}, bf16[512,256]{1,0:T(8,128)(2,1)S(1)}, u32[]{:S(2)}, u32[]{:S(2)}) collective-permute-start(bf16[512,256]{1,0:T(8,128)(2,1)} %param.16), channel_id=1, source_target_pairs={{0,8},{8,0},{16,24},{24,16},{1,9},{9,1},{17,25},{25,17},{2,10},{10... | collective-permute-start | bytes 786440 | tf_op jit(solution)/shard_map/ppermute | solution.py:261
  18.5 2.9 %collective-permute-start.3 = (bf16[512,256]{1,0:T(8,128)(2,1)S(1)}, bf16[512,256]{1,0:T(8,128)(2,1)S(1)}, u32[]{:S(2)}, u32[]{:S(2)}) collective-permute-start(bf16[512,256]{1,0:T(8,128)(2,1)S(1)} %fusion.34), channel_id=1, source_target_pairs={{0,1},{1,0},{2,3},{3,2},{4,5},{5,4},{6,7},{7,6},{8,9},{9,8},{10,11... | collective-permute-start | bytes 786440 | tf_op jit(solution)/shard_map/ppermute | solution.py:261
  18.5 1.9 %collective-permute-start.5 = (bf16[512,256]{1,0:T(8,128)(2,1)S(1)}, bf16[512,256]{1,0:T(8,128)(2,1)S(1)}, u32[]{:S(2)}, u32[]{:S(2)}) collective-permute-start(bf16[512,256]{1,0:T(8,128)(2,1)S(1)} %fusion.37), channel_id=1, source_target_pairs={{0,1},{1,0},{2,3},{3,2},{4,5},{5,4},{6,7},{7,6},{8,9},{9,8},{10,11... | collective-permute-start | bytes 786440 | tf_op jit(solution)/shard_map/ppermute | solution.py:261
  21.2 15.1 %collective-permute-start.6 = (bf16[512,256]{1,0:T(8,128)(2,1)S(1)}, bf16[512,256]{1,0:T(8,128)(2,1)S(1)}, u32[]{:S(2)}, u32[]{:S(2)}) collective-permute-start(bf16[512,256]{1,0:T(8,128)(2,1)S(1)} %fusion.40), channel_id=1, source_target_pairs={{0,1},{1,0},{2,3},{3,2},{4,5},{5,4},{6,7},{7,6},{8,9},{9,8},{10,11... | collective-permute-start | bytes 786440 | tf_op jit(solution)/shard_map/ppermute | solution.py:261
  21.4 26.4 %copy-start = (bf16[512,256]{1,0:T(8,128)(2,1)S(1)}, bf16[512,256]{1,0:T(8,128)(2,1)}, u32[]{:S(2)}) copy-start(bf16[512,256]{1,0:T(8,128)(2,1)} %refs_6_.1) | copy-start | bytes 786436
  21.4 26.4 %copy-start.1 = (bf16[256,256]{1,0:T(8,128)(2,1)S(1)}, bf16[256,256]{1,0:T(8,128)(2,1)}, u32[]{:S(2)}) copy-start(bf16[256,256]{1,0:T(8,128)(2,1)} %refs_4_.1) | copy-start | bytes 393220
  21.4 26.4 %copy-start.2 = (f32[256]{0:T(256)S(1)}, f32[256]{0:T(256)}, u32[]{:S(2)}) copy-start(f32[256]{0:T(256)} %param.18) | copy-start | bytes 3076
  21.5 8.6 %collective-permute-start.4 = (bf16[512,256]{1,0:T(8,128)(2,1)S(1)}, bf16[512,256]{1,0:T(8,128)(2,1)S(1)}, u32[]{:S(2)}, u32[]{:S(2)}) collective-permute-start(bf16[512,256]{1,0:T(8,128)(2,1)S(1)} %add_convert_fusion), channel_id=1, source_target_pairs={{0,2},{1,3},{2,0},{3,1},{4,6},{5,7},{6,4},{7,5},{8,10},{9,11},{10,... | collective-permute-start | bytes 786440 | tf_op jit(solution)/shard_map/ppermute | solution.py:261
  23.8 10.1 %collective-permute-start.7 = (bf16[512,256]{1,0:T(8,128)(2,1)S(1)}, bf16[512,256]{1,0:T(8,128)(2,1)S(1)}, u32[]{:S(2)}, u32[]{:S(2)}) collective-permute-start(bf16[512,256]{1,0:T(8,128)(2,1)S(1)} %fusion.43), channel_id=1, source_target_pairs={{0,1},{1,0},{2,3},{3,2},{4,5},{5,4},{6,7},{7,6},{8,9},{9,8},{10,11... | collective-permute-start | bytes 786440 | tf_op jit(solution)/shard_map/ppermute | solution.py:261
  24.0 13.0 %collective-permute-start.10 = (bf16[512,256]{1,0:T(8,128)(2,1)S(1)}, bf16[512,256]{1,0:T(8,128)(2,1)S(1)}, u32[]{:S(2)}, u32[]{:S(2)}) collective-permute-start(bf16[512,256]{1,0:T(8,128)(2,1)S(1)} %add_convert_fusion), channel_id=1, source_target_pairs={{2,4},{3,5},{4,2},{5,3},{10,12},{11,13},{12,10},{13,11},{18,20},{1... | collective-permute-start | bytes 786440 | tf_op jit(solution)/shard_map/ppermute | solution.py:266
  30.8 17.0 %collective-permute-start.9 = (bf16[512,256]{1,0:T(8,128)(2,1)S(1)}, bf16[512,256]{1,0:T(8,128)(2,1)S(1)}, u32[]{:S(2)}, u32[]{:S(2)}) collective-permute-start(bf16[512,256]{1,0:T(8,128)(2,1)S(1)} %fusion.31), channel_id=1, source_target_pairs={{0,4},{1,5},{2,6},{3,7},{4,0},{5,1},{6,2},{7,3},{8,12},{9,13},{10,... | collective-permute-start | bytes 786440 | tf_op jit(solution)/shard_map/ppermute | solution.py:261
  34.6 13.2 %collective-permute-start.8 = (bf16[512,256]{1,0:T(8,128)(2,1)S(1)}, bf16[512,256]{1,0:T(8,128)(2,1)S(1)}, u32[]{:S(2)}, u32[]{:S(2)}) collective-permute-start(bf16[512,256]{1,0:T(8,128)(2,1)S(1)} %fusion.28), channel_id=1, source_target_pairs={{0,2},{1,3},{2,0},{3,1},{4,6},{5,7},{6,4},{7,5},{8,10},{9,11},{10,... | collective-permute-start | bytes 786440 | tf_op jit(solution)/shard_map/ppermute | solution.py:261
  48.9 14.6 %collective-permute-start.21 = (f32[272,256]{1,0:T(8,128)S(1)}, f32[272,256]{1,0:T(8,128)S(1)}, u32[]{:S(2)}, u32[]{:S(2)}) collective-permute-start(f32[272,256]{1,0:T(8,128)S(1)} %get-tuple-element.85), channel_id=1, source_target_pairs={{0,1},{1,0},{2,3},{3,2},{4,5},{5,4},{6,7},{7,6},{8,9},{9,8},{10,11... | collective-permute-start | bytes 835592 | tf_op jit(solution)/shard_map/ppermute | solution.py:261
  48.9 14.6 %collective-permute-start.14 = (bf16[256,512]{1,0:T(8,128)(2,1)S(1)}, bf16[256,512]{1,0:T(8,128)(2,1)S(1)}, u32[]{:S(2)}, u32[]{:S(2)}) collective-permute-start(bf16[256,512]{1,0:T(8,128)(2,1)S(1)} %get-tuple-element.78.refs_1_), channel_id=1, source_target_pairs={{0,4},{1,5},{2,6},{3,7},{4,0},{5,1},{6,2},{7,3},{8,12},{9,13},{10,... | collective-permute-start | bytes 786440 | tf_op jit(solution)/shard_map/ppermute | solution.py:261
  48.9 14.7 %collective-permute-start.12 = (bf16[256,512]{1,0:T(8,128)(2,1)S(1)}, bf16[256,512]{1,0:T(8,128)(2,1)S(1)}, u32[]{:S(2)}, u32[]{:S(2)}) collective-permute-start(bf16[256,512]{1,0:T(8,128)(2,1)S(1)} %get-tuple-element.78.refs_1_), channel_id=1, source_target_pairs={{0,2},{1,3},{2,0},{3,1},{4,6},{5,7},{6,4},{7,5},{8,10},{9,11},{10,... | collective-permute-start | bytes 786440 | tf_op jit(solution)/shard_map/ppermute | solution.py:261
  51.3 18.4 %collective-permute-start.17 = (bf16[256,512]{1,0:T(8,128)(2,1)S(1)}, bf16[256,512]{1,0:T(8,128)(2,1)S(1)}, u32[]{:S(2)}, u32[]{:S(2)}) collective-permute-start(bf16[256,512]{1,0:T(8,128)(2,1)S(1)} %get-tuple-element.78.refs_1_), channel_id=1, source_target_pairs={{2,4},{3,5},{4,2},{5,3},{10,12},{11,13},{12,10},{13,11},{18,20},{1... | collective-permute-start | bytes 786440 | tf_op jit(solution)/shard_map/ppermute | solution.py:266
  52.2 19.6 %collective-permute-start.11 = (bf16[256,512]{1,0:T(8,128)(2,1)S(1)}, bf16[256,512]{1,0:T(8,128)(2,1)S(1)}, u32[]{:S(2)}, u32[]{:S(2)}) collective-permute-start(bf16[256,512]{1,0:T(8,128)(2,1)S(1)} %get-tuple-element.78.refs_1_), channel_id=1, source_target_pairs={{0,1},{1,0},{2,3},{3,2},{4,5},{5,4},{6,7},{7,6},{8,9},{9,8},{10,11... | collective-permute-start | bytes 786440 | tf_op jit(solution)/shard_map/ppermute | solution.py:261
  63.5 8.2 %collective-permute-start.16 = (bf16[256,512]{1,0:T(8,128)(2,1)S(1)}, bf16[256,512]{1,0:T(8,128)(2,1)S(1)}, u32[]{:S(2)}, u32[]{:S(2)}) collective-permute-start(bf16[256,512]{1,0:T(8,128)(2,1)S(1)} %collective-permute-done.14.refs_3_), channel_id=1, source_target_pairs={{0,2},{1,3},{2,0},{3,1},{4,6},{5,7},{6,4},{7,5},{8,10},{9,11},{10,... | collective-permute-start | bytes 786440 | tf_op jit(solution)/shard_map/ppermute | solution.py:261
  63.5 8.3 %collective-permute-start.15 = (bf16[256,512]{1,0:T(8,128)(2,1)S(1)}, bf16[256,512]{1,0:T(8,128)(2,1)S(1)}, u32[]{:S(2)}, u32[]{:S(2)}) collective-permute-start(bf16[256,512]{1,0:T(8,128)(2,1)S(1)} %collective-permute-done.14.refs_3_), channel_id=1, source_target_pairs={{0,1},{1,0},{2,3},{3,2},{4,5},{5,4},{6,7},{7,6},{8,9},{9,8},{10,11... | collective-permute-start | bytes 786440 | tf_op jit(solution)/shard_map/ppermute | solution.py:261
  63.7 6.0 %collective-permute-start.22 = (bf16[272,256]{1,0:T(8,128)(2,1)S(1)}, bf16[272,256]{1,0:T(8,128)(2,1)S(1)}, u32[]{:S(2)}, u32[]{:S(2)}) collective-permute-start(bf16[272,256]{1,0:T(8,128)(2,1)S(1)} %add_convert_fusion.4), channel_id=1, source_target_pairs={{0,8},{8,0},{16,24},{24,16},{1,9},{9,1},{17,25},{25,17},{2,10},{10... | collective-permute-start | bytes 417800 | tf_op jit(solution)/shard_map/ppermute | solution.py:261
  69.7 2.1 %collective-permute-start.13 = (bf16[256,512]{1,0:T(8,128)(2,1)S(1)}, bf16[256,512]{1,0:T(8,128)(2,1)S(1)}, u32[]{:S(2)}, u32[]{:S(2)}) collective-permute-start(bf16[256,512]{1,0:T(8,128)(2,1)S(1)} %collective-permute-done.12.refs_2_), channel_id=1, source_target_pairs={{0,1},{1,0},{2,3},{3,2},{4,5},{5,4},{6,7},{7,6},{8,9},{9,8},{10,11... | collective-permute-start | bytes 786440 | tf_op jit(solution)/shard_map/ppermute | solution.py:261
  69.8 6.1 %collective-permute-start.23 = (bf16[272,256]{1,0:T(8,128)(2,1)S(1)}, bf16[272,256]{1,0:T(8,128)(2,1)S(1)}, u32[]{:S(2)}, u32[]{:S(2)}) collective-permute-start(bf16[272,256]{1,0:T(8,128)(2,1)S(1)} %add_convert_fusion.3), channel_id=1, source_target_pairs={{0,16},{8,24},{16,0},{24,8},{1,17},{9,25},{17,1},{25,9},{2,18},{10... | collective-permute-start | bytes 417800 | tf_op jit(solution)/shard_map/ppermute | solution.py:261
  71.7 4.2 %collective-permute-start.18 = (bf16[256,512]{1,0:T(8,128)(2,1)S(1)}, bf16[256,512]{1,0:T(8,128)(2,1)S(1)}, u32[]{:S(2)}, u32[]{:S(2)}) collective-permute-start(bf16[256,512]{1,0:T(8,128)(2,1)S(1)} %broadcast_select_fusion.refs_1_), channel_id=1, source_target_pairs={{0,1},{1,0},{2,3},{3,2},{4,5},{5,4},{6,7},{7,6},{8,9},{9,8},{10,11... | collective-permute-start | bytes 786440 | tf_op jit(solution)/shard_map/ppermute | solution.py:261
  77.3 6.2 %collective-permute-start.25 = (bf16[272,256]{1,0:T(8,128)(2,1)S(1)}, bf16[272,256]{1,0:T(8,128)(2,1)S(1)}, u32[]{:S(2)}, u32[]{:S(2)}) collective-permute-start(bf16[272,256]{1,0:T(8,128)(2,1)S(1)} %add_convert_fusion.2), channel_id=1, source_target_pairs={{0,2},{1,3},{2,0},{3,1},{4,6},{5,7},{6,4},{7,5},{8,10},{9,11},{10,... | collective-permute-start | bytes 417800 | tf_op jit(solution)/shard_map/ppermute | solution.py:261
  79.3 10.2 %collective-permute-start.19 = (bf16[512,256]{1,0:T(8,128)(2,1)S(1)}, bf16[512,256]{1,0:T(8,128)(2,1)S(1)}, u32[]{:S(2)}, u32[]{:S(2)}) collective-permute-start(bf16[512,256]{1,0:T(8,128)(2,1)S(1)} %back_last.3), channel_id=1, source_target_pairs={{0,24},{8,16},{16,8},{24,0},{1,25},{9,17},{17,9},{25,1},{2,26},{10... | collective-permute-start | bytes 786440 | tf_op jit(solution)/shard_map/ppermute | solution.py:261
  80.6 12.5 %collective-permute-start.24 = (bf16[512,256]{1,0:T(8,128)(2,1)S(1)}, bf16[512,256]{1,0:T(8,128)(2,1)S(1)}, u32[]{:S(2)}, u32[]{:S(2)}) collective-permute-start(bf16[512,256]{1,0:T(8,128)(2,1)S(1)} %get-tuple-element.87), channel_id=1, source_target_pairs={{0,8},{8,0},{16,24},{24,16},{1,9},{9,1},{17,25},{25,17},{2,10},{10... | collective-permute-start | bytes 786440 | tf_op jit(solution)/shard_map/ppermute | solution.py:261
  81.8 11.7 %collective-permute-start.20 = (bf16[512,256]{1,0:T(8,128)(2,1)S(1)}, bf16[512,256]{1,0:T(8,128)(2,1)S(1)}, u32[]{:S(2)}, u32[]{:S(2)}) collective-permute-start(bf16[512,256]{1,0:T(8,128)(2,1)S(1)} %get-tuple-element.84), channel_id=1, source_target_pairs={{0,16},{8,24},{16,0},{24,8},{1,17},{9,25},{17,1},{25,9},{2,18},{10... | collective-permute-start | bytes 786440 | tf_op jit(solution)/shard_map/ppermute | solution.py:261
  83.5 10.2 %collective-permute-start.26 = (bf16[272,256]{1,0:T(8,128)(2,1)S(1)}, bf16[272,256]{1,0:T(8,128)(2,1)S(1)}, u32[]{:S(2)}, u32[]{:S(2)}) collective-permute-start(bf16[272,256]{1,0:T(8,128)(2,1)S(1)} %add_convert_fusion.1.refs_1_), channel_id=1, source_target_pairs={{0,4},{1,5},{2,6},{3,7},{4,0},{5,1},{6,2},{7,3},{8,12},{9,13},{10,... | collective-permute-start | bytes 417800 | tf_op jit(solution)/shard_map/ppermute | solution.py:261
where the time goes:
time: 94.7 us; the launch traced here: 94.5 us
  waiting for transfers between devices  46.5 us (49%)
  starting transfers between devices  25.5 us (27%)
  Pallas kernels  13.8 us (15%)
  matrix products  5.67 us (6%)
  between operations  1.58 us (2%)
  local copies, waits for them, and re-layouts  1.09 us (1%)
    ppermute x25, waiting for transfers between devices, swap(): return lax.ppermute(value, axis, [(i, i ^ mask) for i in range(count)])  46.5 us
    ppermute x25, starting transfers between devices, swap(): return lax.ppermute(value, axis, [(i, i ^ mask) for i in range(count)])  24 us
    pallas_call x1, Pallas kernels, densify(): pl.pallas_call(lambda *refs: densify_kernel(per, col_count // 2, bands ==...  6.44 us
    dot_general x8, matrix products, cell_product(): return jnp.dot(cell_rows(core, k), source, preferred_element_type=F32)  5.67 us
    pallas_call x5, Pallas kernels, back(): pl.pallas_call(lambda *refs: back_kernel(panels, chosen, last, total is n...  5.43 us
  transfers between devices with their start and end apart: 27, of which 13 were waited for; matrix products, arithmetic and copies ran while one was open for 6% of the time, Pallas kernels for 11%

commit v1 on v0

--- a/solution.py
+++ b/solution.py
@@ -139,11 +139,11 @@
     width = weight.shape[0]
     local_ref[:width] = lax.dot_general(
         aggregated, grad_pre, (((0,), (0,)), ((), ())), preferred_element_type=F32
-    )
+    ).astype(BF16)
     local_ref[width:] = jnp.broadcast_to(
         jnp.sum(grad_pre.astype(F32), axis=0, keepdims=True),
         (local_ref.shape[0] - width, width),
-    )
+    ).astype(BF16)
 
 
 def dense(own, parts, weight, bias, cotangent):
@@ -152,7 +152,7 @@
     shapes = (
         jax.ShapeDtypeStruct((nodes, width), BF16),
         jax.ShapeDtypeStruct((width, nodes), BF16),
-        jax.ShapeDtypeStruct((width + 16, width), F32),
+        jax.ShapeDtypeStruct((width + 16, width), BF16),
     )
     return pl.pallas_call(
         lambda *refs: dense_kernel(len(parts), *refs),
@@ -280,14 +280,14 @@
     return [near, across, middle], chunk(0, both)
 
 
-def gather_far(value, count):
+def gather_far(value, count, hold):
     if count != 4:
-        return [value] + [swap(value, "col", 2 * k) for k in range(1, count)]
-    across = swap(value, "col", 4)
+        return [value] + [swap(value, "col", 2 * k) for k in range(1, count)], hold
+    across, hold = lax.optimization_barrier((swap(value, "col", 4), hold))
     near = swap(value, "col", 2)
     passed = swap(across, "col", 2)
     middle = move(value, [(1, 2), (2, 1)])
-    return [value, near, across, jnp.where(at_end(), passed, middle)]
+    return [value, near, across, jnp.where(at_end(), passed, middle)], hold
 
 
 def at_end():
@@ -297,8 +297,8 @@
 
 def sum_over(value, axis, masks):
     for mask in masks:
-        value = value.astype(BF16)
         value = value.astype(F32) + swap(value, axis, mask).astype(F32)
+        value = lax.optimization_barrier(value.astype(BF16))
     return value
 
 
@@ -347,9 +347,11 @@
     parts, own = sum_far(own_far, chunk, from_mate[far - 1])
     hidden, grad_agg, local = dense(own, parts, weight, bias, cotangent)
 
-    part = local + swap(local, "col", 1)
-    part = sum_over(part, "row", doublings(1, row_count)).astype(BF16)
-    own_grads = gather_far(grad_agg, half)
+    first, *masks = doublings(1, row_count)
+    part = sum_over(local, "row", [first])
+    own_grads, part = gather_far(grad_agg, half, part)
+    part = sum_over(part, "row", masks)
+    part = sum_over(part, "col", [1])
     mate_grads = [swap(grads, "col", 1) for grads in own_grads[:far]]
 
     if cell.size * 2 <= CELL_IN_VMEM:
@@ -376,7 +378,7 @@
     part, pieces[1] = lax.optimization_barrier((part, pieces[1]))
     landed = [swap(pieces[k], "row", k) for k in range(row_count - 1, 0, -1)]
     *masks, mask = doublings(2, col_count)
-    part = sum_over(part, "col", masks).astype(BF16)
+    part = sum_over(part, "col", masks)
     value = pieces[0]
     for piece in landed:
         value = value + piece.astype(F32)

time: 94.7 us -> 92.1 us (0.973)
  waiting for transfers between devices: 46.5 us -> 44.5 us
  starting transfers between devices: 25.5 us -> 24.4 us
    ppermute x25, waiting for transfers between devices: 46.5 us -> 44.5 us  [swap(): return lax.ppermute(value, axis, [(i, i ^ mask) for i in range(count)])]
    ppermute x25, starting transfers between devices: 24 us -> 22.9 us  [swap(): return lax.ppermute(value, axis, [(i, i ^ mask) for i in range(count)])]
  transfers between devices with their start and end apart: 27 -> 27, of which waited for: 13 -> 14; matrix products, arithmetic and copies ran while one was open for 6% -> 6% of each run, Pallas kernels for 11% -> 12%
where the time goes in v1:
time: 92.1 us; the launch traced here: 91.9 us
  waiting for transfers between devices  44.5 us (48%)
  starting transfers between devices  24.4 us (26%)
  Pallas kernels  14.3 us (16%)
  matrix products  5.67 us (6%)
  between operations  1.6 us (2%)
  local copies, waits for them, and re-layouts  1.09 us (1%)
    ppermute x25, waiting for transfers between devices, swap(): return lax.ppermute(value, axis, [(i, i ^ mask) for i in range(count)])  44.5 us
    ppermute x25, starting transfers between devices, swap(): return lax.ppermute(value, axis, [(i, i ^ mask) for i in range(count)])  22.9 us
    pallas_call x1, Pallas kernels, densify(): pl.pallas_call(lambda *refs: densify_kernel(per, col_count // 2, bands ==...  6.94 us
    dot_general x8, matrix products, cell_product(): return jnp.dot(cell_rows(core, k), source, preferred_element_type=F32)  5.67 us
    pallas_call x5, Pallas kernels, back(): pl.pallas_call(lambda *refs: back_kernel(panels, chosen, last, total is n...  5.43 us
  transfers between devices with their start and end apart: 27, of which 14 were waited for; matrix products, arithmetic and copies ran while one was open for 6% of the time, Pallas kernels for 12%

profile of v1, /device:TPU:0, one launch (start us, length us, event | category | flops | bytes accessed | tf_op | source)
XLA Modules:
  0.0 91.9 jit_solution(567468346975642564)
XLA Ops:
  0.6 4.0 %collective-permute-start = (bf16[512,256]{1,0:T(8,128)(2,1)}, bf16[512,256]{1,0:T(8,128)(2,1)S(1)}, u32[]{:S(2)}, u32[]{:S(2)}) collective-permute-start(bf16[512,256]{1,0:T(8,128)(2,1)} %param.16), channel_id=1, source_target_pairs={{0,24},{8,16},{16,8},{24,0},{1,25},{9,17},{17,9},{25,1},{2,26},{10... | collective-permute-start | bytes 786440 | tf_op jit(solution)/shard_map/ppermute | solution.py:261
  4.6 0.5 collective-permute-start.1
  5.9 1.0 %scatter.14 = bf16[2048,256]{1,0:T(8,128)(2,1)S(1)} pad(bf16[512,256]{1,0:T(8,128)(2,1)} %param.16, bf16[]{:T(256)} %constant.127.clone.1), padding=0_1536x0_0 | pad | bytes 1310722 | tf_op jit(solution)/shard_map/scatter | solution.py:317
  6.9 6.9 %densify.1.refs_0_ = bf16[4096,2048]{1,0:T(8,128)(2,1)S(1)} custom-call(s32[1,1,384]{2,1,0:T(1,128)} %refs_0_.1, s32[1,1,384]{2,1,0:T(1,128)} %refs_1_.1, s32[1,1]{1,0:T(1,128)S(6)} %copy.15.refs_2_, bf16[384,128,128]{2,1,0:T(8,128)(2,1)} %bitcast.12, bf16[384,128,128]{2,1,0:T(8,128)(2,1)} %bitcast.13, bf16[384,128,128]{2,1,0:T(8,128)(2,1)} %bitcast.14), custom_call_target="tpu_custom_call" | custom-call | bytes 33554432 | tf_op jit(solution)/shard_map/densify/pallas_call | solution.py:93
  13.9 2.8 %collective-permute-done.1 = bf16[512,256]{1,0:T(8,128)(2,1)S(1)} collective-permute-done((bf16[512,256]{1,0:T(8,128)(2,1)}, bf16[512,256]{1,0:T(8,128)(2,1)S(1)}, u32[]{:S(2)}, u32[]{:S(2)}) %collective-permute-start.1) | collective-permute-done | bytes 262176 | tf_op jit(solution)/shard_map/ppermute | solution.py:261
  16.7 0.3 collective-permute-done.2
  17.0 0.7 fusion.37
  17.8 0.7 fusion.34
  18.5 0.5 collective-permute-start.5
  19.0 0.7 fusion.10
  19.8 0.7 collective-permute-done.5
  20.4 0.7 fusion.40
  21.2 0.2 collective-permute-start.6
  21.5 1.7 %collective-permute-start.4 = (bf16[512,256]{1,0:T(8,128)(2,1)S(1)}, bf16[512,256]{1,0:T(8,128)(2,1)S(1)}, u32[]{:S(2)}, u32[]{:S(2)}) collective-permute-start(bf16[512,256]{1,0:T(8,128)(2,1)S(1)} %add_convert_fusion), channel_id=1, source_target_pairs={{0,2},{1,3},{2,0},{3,1},{4,6},{5,7},{6,4},{7,5},{8,10},{9,11},{10,... | collective-permute-start | bytes 786440 | tf_op jit(solution)/shard_map/ppermute | solution.py:261
  23.1 0.7 fusion.43
  24.0 0.7 collective-permute-start.10
  24.6 5.5 %collective-permute-done.4 = bf16[512,256]{1,0:T(8,128)(2,1)S(1)} collective-permute-done((bf16[512,256]{1,0:T(8,128)(2,1)S(1)}, bf16[512,256]{1,0:T(8,128)(2,1)S(1)}, u32[]{:S(2)}, u32[]{:S(2)}) %collective-permute-start.4) | collective-permute-done | bytes 262176 | tf_op jit(solution)/shard_map/ppermute | solution.py:261
  30.1 0.7 fusion.31
  30.8 2.6 %collective-permute-start.9 = (bf16[512,256]{1,0:T(8,128)(2,1)S(1)}, bf16[512,256]{1,0:T(8,128)(2,1)S(1)}, u32[]{:S(2)}, u32[]{:S(2)}) collective-permute-start(bf16[512,256]{1,0:T(8,128)(2,1)S(1)} %fusion.31), channel_id=1, source_target_pairs={{0,4},{1,5},{2,6},{3,7},{4,0},{5,1},{6,2},{7,3},{8,12},{9,13},{10,... | collective-permute-start | bytes 786440 | tf_op jit(solution)/shard_map/ppermute | solution.py:261
  33.5 0.7 fusion.28
  34.2 1.6 %collective-permute-start.8 = (bf16[512,256]{1,0:T(8,128)(2,1)S(1)}, bf16[512,256]{1,0:T(8,128)(2,1)S(1)}, u32[]{:S(2)}, u32[]{:S(2)}) collective-permute-start(bf16[512,256]{1,0:T(8,128)(2,1)S(1)} %fusion.28), channel_id=1, source_target_pairs={{0,2},{1,3},{2,0},{3,1},{4,6},{5,7},{6,4},{7,5},{8,10},{9,11},{10,... | collective-permute-start | bytes 786440 | tf_op jit(solution)/shard_map/ppermute | solution.py:261
  35.8 0.7 fusion.16.refs_0_
  36.6 10.8 %collective-permute-done.8.refs_1_ = bf16[512,256]{1,0:T(8,128)(2,1)S(1)} collective-permute-done((bf16[512,256]{1,0:T(8,128)(2,1)S(1)}, bf16[512,256]{1,0:T(8,128)(2,1)S(1)}, u32[]{:S(2)}, u32[]{:S(2)}) %collective-permute-start.8) | collective-permute-done | bytes 262176 | tf_op jit(solution)/shard_map/ppermute | solution.py:261
  47.4 1.1 %dense.1 = (bf16[512,256]{1,0:T(8,128)(2,1)}, bf16[256,512]{1,0:T(8,128)(2,1)S(1)}, bf16[272,256]{1,0:T(8,128)(2,1)S(1)}) custom-call(f32[512,256]{1,0:T(8,128)S(1)} %fusion.16.refs_0_, bf16[512,256]{1,0:T(8,128)(2,1)S(1)} %collective-permute-done.8.refs_1_, bf16[512,256]{1,0:T(8,128)(2,1)S(1)} %collective-permute-done.9.refs_2_, ...), custom_call_target="tpu_custom_call" | custom-call | flops 201326592 | bytes 1048576 | tf_op jit(solution)/shard_map/dense/pallas_call | solution.py:157
  48.5 1.5 %collective-permute-start.15 = (bf16[272,256]{1,0:T(8,128)(2,1)S(1)}, bf16[272,256]{1,0:T(8,128)(2,1)S(1)}, u32[]{:S(2)}, u32[]{:S(2)}) collective-permute-start(bf16[272,256]{1,0:T(8,128)(2,1)S(1)} %get-tuple-element.81), channel_id=1, source_target_pairs={{0,8},{8,0},{16,24},{24,16},{1,9},{9,1},{17,25},{25,17},{2,10},{10... | collective-permute-start | bytes 417800 | tf_op jit(solution)/shard_map/ppermute | solution.py:261
  50.0 2.4 %collective-permute-start.12 = (bf16[256,512]{1,0:T(8,128)(2,1)S(1)}, bf16[256,512]{1,0:T(8,128)(2,1)S(1)}, u32[]{:S(2)}, u32[]{:S(2)}) collective-permute-start(bf16[256,512]{1,0:T(8,128)(2,1)S(1)} %get-tuple-element.80.refs_1_), channel_id=1, source_target_pairs={{0,2},{1,3},{2,0},{3,1},{4,6},{5,7},{6,4},{7,5},{8,10},{9,11},{10,... | collective-permute-start | bytes 786440 | tf_op jit(solution)/shard_map/ppermute | solution.py:261
  52.4 0.8 collective-permute-start.18
  53.3 0.2 collective-permute-done.15
  53.6 9.9 %collective-permute-done.14.refs_3_ = bf16[256,512]{1,0:T(8,128)(2,1)S(1)} collective-permute-done((bf16[256,512]{1,0:T(8,128)(2,1)S(1)}, bf16[256,512]{1,0:T(8,128)(2,1)S(1)}, u32[]{:S(2)}, u32[]{:S(2)}) %collective-permute-start.14) | collective-permute-done | bytes 262176 | tf_op jit(solution)/shard_map/ppermute | solution.py:261
  63.6 0.8 collective-permute-start.22
  64.4 1.8 %back.2.refs_4_ = f32[256,2048]{1,0:T(8,128)S(1)} custom-call(bf16[4096,2048]{1,0:T(8,128)(2,1)S(1)} %densify.1.refs_0_, bf16[256,512]{1,0:T(8,128)(2,1)S(1)} %get-tuple-element.80.refs_1_, bf16[256,512]{1,0:T(8,128)(2,1)S(1)} %collective-permute-done.12.refs_2_, bf16[256,512]{1,0:T(8,128)(2,1)S(1)} %collective-permute-done.14.refs_3_), custom_call_target="tpu_custom_call" | custom-call | flops 1610612736 | bytes 3145728 | tf_op jit(solution)/shard_map/back/pallas_call | solution.py:218
  66.2 3.3 %collective-permute-done.22 = bf16[272,256]{1,0:T(8,128)(2,1)S(1)} collective-permute-done((bf16[272,256]{1,0:T(8,128)(2,1)S(1)}, bf16[272,256]{1,0:T(8,128)(2,1)S(1)}, u32[]{:S(2)}, u32[]{:S(2)}) %collective-permute-start.22) | collective-permute-done | bytes 139296 | tf_op jit(solution)/shard_map/ppermute | solution.py:261
  69.6 0.6 collective-permute-start.23
  70.2 1.4 %collective-permute-done.17 = bf16[256,512]{1,0:T(8,128)(2,1)S(1)} collective-permute-done((bf16[256,512]{1,0:T(8,128)(2,1)S(1)}, bf16[256,512]{1,0:T(8,128)(2,1)S(1)}, u32[]{:S(2)}, u32[]{:S(2)}) %collective-permute-start.17) | collective-permute-done | bytes 262176 | tf_op jit(solution)/shard_map/ppermute | solution.py:261
  71.7 1.8 %back.3.refs_3_ = f32[256,2048]{1,0:T(8,128)S(1)} custom-call(bf16[4096,2048]{1,0:T(8,128)(2,1)S(1)} %densify.1.refs_0_, bf16[256,512]{1,0:T(8,128)(2,1)S(1)} %collective-permute-done.11.refs_1_, bf16[256,512]{1,0:T(8,128)(2,1)S(1)} %collective-permute-done.13.refs_2_, bf16[256,512]{1,0:T(8,128)(2,1)S(1)} %collective-permute-done.16.refs_3_, ...), custom_call_target="tpu_custom_call" | custom-call | flops 1610612736 | bytes 3145728 | tf_op jit(solution)/shard_map/back/pallas_call | solution.py:218
  73.6 0.5 back_last.3
  74.1 0.8 back_last.4
  74.9 1.4 %collective-permute-start.25 = (bf16[272,256]{1,0:T(8,128)(2,1)S(1)}, bf16[272,256]{1,0:T(8,128)(2,1)S(1)}, u32[]{:S(2)}, u32[]{:S(2)}) collective-permute-start(bf16[272,256]{1,0:T(8,128)(2,1)S(1)} %add_convert_fusion.2), channel_id=1, source_target_pairs={{0,2},{1,3},{2,0},{3,1},{4,6},{5,7},{6,4},{7,5},{8,10},{9,11},{10,... | collective-permute-start | bytes 417800 | tf_op jit(solution)/shard_map/ppermute | solution.py:261
  76.3 1.4 %collective-permute-start.20 = (bf16[512,256]{1,0:T(8,128)(2,1)S(1)}, bf16[512,256]{1,0:T(8,128)(2,1)S(1)}, u32[]{:S(2)}, u32[]{:S(2)}) collective-permute-start(bf16[512,256]{1,0:T(8,128)(2,1)S(1)} %back_last.3), channel_id=1, source_target_pairs={{0,24},{8,16},{16,8},{24,0},{1,25},{9,17},{17,9},{25,1},{2,26},{10... | collective-permute-start | bytes 786440 | tf_op jit(solution)/shard_map/ppermute | solution.py:261
  77.8 0.9 %collective-permute-start.24 = (bf16[512,256]{1,0:T(8,128)(2,1)S(1)}, bf16[512,256]{1,0:T(8,128)(2,1)S(1)}, u32[]{:S(2)}, u32[]{:S(2)}) collective-permute-start(bf16[512,256]{1,0:T(8,128)(2,1)S(1)} %get-tuple-element.91), channel_id=1, source_target_pairs={{0,8},{8,0},{16,24},{24,16},{1,9},{9,1},{17,25},{25,17},{2,10},{10... | collective-permute-start | bytes 786440 | tf_op jit(solution)/shard_map/ppermute | solution.py:261
  78.7 1.1 %collective-permute-start.21 = (bf16[512,256]{1,0:T(8,128)(2,1)S(1)}, bf16[512,256]{1,0:T(8,128)(2,1)S(1)}, u32[]{:S(2)}, u32[]{:S(2)}) collective-permute-start(bf16[512,256]{1,0:T(8,128)(2,1)S(1)} %get-tuple-element.88), channel_id=1, source_target_pairs={{0,16},{8,24},{16,0},{24,8},{1,17},{9,25},{17,1},{25,9},{2,18},{10... | collective-permute-start | bytes 786440 | tf_op jit(solution)/shard_map/ppermute | solution.py:261
  79.8 0.6 back_last.5
  80.4 0.6 collective-permute-done.25
  81.1 1.0 %collective-permute-start.26 = (bf16[272,256]{1,0:T(8,128)(2,1)S(1)}, bf16[272,256]{1,0:T(8,128)(2,1)S(1)}, u32[]{:S(2)}, u32[]{:S(2)}) collective-permute-start(bf16[272,256]{1,0:T(8,128)(2,1)S(1)} %add_convert_fusion.1.refs_1_), channel_id=1, source_target_pairs={{0,4},{1,5},{2,6},{3,7},{4,0},{5,1},{6,2},{7,3},{8,12},{9,13},{10,... | collective-permute-start | bytes 417800 | tf_op jit(solution)/shard_map/ppermute | solution.py:261
  82.1 4.4 %collective-permute-done.20 = bf16[512,256]{1,0:T(8,128)(2,1)S(1)} collective-permute-done((bf16[512,256]{1,0:T(8,128)(2,1)S(1)}, bf16[512,256]{1,0:T(8,128)(2,1)S(1)}, u32[]{:S(2)}, u32[]{:S(2)}) %collective-permute-start.20) | collective-permute-done | bytes 262176 | tf_op jit(solution)/shard_map/ppermute | solution.py:261
  86.5 3.9 %collective-permute-done.24 = bf16[512,256]{1,0:T(8,128)(2,1)S(1)} collective-permute-done((bf16[512,256]{1,0:T(8,128)(2,1)S(1)}, bf16[512,256]{1,0:T(8,128)(2,1)S(1)}, u32[]{:S(2)}, u32[]{:S(2)}) %collective-permute-start.24) | collective-permute-done | bytes 262176 | tf_op jit(solution)/shard_map/ppermute | solution.py:261
  90.4 0.5 collective-permute-done.21
  91.1 0.8 finish.1
  (39 shorter events, 1.1 us)
Async XLA Ops:
  0.6 13.2 %collective-permute-start = (bf16[512,256]{1,0:T(8,128)(2,1)}, bf16[512,256]{1,0:T(8,128)(2,1)S(1)}, u32[]{:S(2)}, u32[]{:S(2)}) collective-permute-start(bf16[512,256]{1,0:T(8,128)(2,1)} %param.16), channel_id=1, source_target_pairs={{0,24},{8,16},{16,8},{24,0},{1,25},{9,17},{17,9},{25,1},{2,26},{10... | collective-permute-start | bytes 786440 | tf_op jit(solution)/shard_map/ppermute | solution.py:261
  4.6 12.1 %collective-permute-start.1 = (bf16[512,256]{1,0:T(8,128)(2,1)}, bf16[512,256]{1,0:T(8,128)(2,1)S(1)}, u32[]{:S(2)}, u32[]{:S(2)}) collective-permute-start(bf16[512,256]{1,0:T(8,128)(2,1)} %param.16), channel_id=1, source_target_pairs={{0,16},{8,24},{16,0},{24,8},{1,17},{9,25},{17,1},{25,9},{2,18},{10... | collective-permute-start | bytes 786440 | tf_op jit(solution)/shard_map/ppermute | solution.py:261
  5.1 11.9 %collective-permute-start.2 = (bf16[512,256]{1,0:T(8,128)(2,1)}, bf16[512,256]{1,0:T(8,128)(2,1)S(1)}, u32[]{:S(2)}, u32[]{:S(2)}) collective-permute-start(bf16[512,256]{1,0:T(8,128)(2,1)} %param.16), channel_id=1, source_target_pairs={{0,8},{8,0},{16,24},{24,16},{1,9},{9,1},{17,25},{25,17},{2,10},{10... | collective-permute-start | bytes 786440 | tf_op jit(solution)/shard_map/ppermute | solution.py:261
  18.5 2.9 %collective-permute-start.3 = (bf16[512,256]{1,0:T(8,128)(2,1)S(1)}, bf16[512,256]{1,0:T(8,128)(2,1)S(1)}, u32[]{:S(2)}, u32[]{:S(2)}) collective-permute-start(bf16[512,256]{1,0:T(8,128)(2,1)S(1)} %fusion.34), channel_id=1, source_target_pairs={{0,1},{1,0},{2,3},{3,2},{4,5},{5,4},{6,7},{7,6},{8,9},{9,8},{10,11... | collective-permute-start | bytes 786440 | tf_op jit(solution)/shard_map/ppermute | solution.py:261
  18.5 1.9 %collective-permute-start.5 = (bf16[512,256]{1,0:T(8,128)(2,1)S(1)}, bf16[512,256]{1,0:T(8,128)(2,1)S(1)}, u32[]{:S(2)}, u32[]{:S(2)}) collective-permute-start(bf16[512,256]{1,0:T(8,128)(2,1)S(1)} %fusion.37), channel_id=1, source_target_pairs={{0,1},{1,0},{2,3},{3,2},{4,5},{5,4},{6,7},{7,6},{8,9},{9,8},{10,11... | collective-permute-start | bytes 786440 | tf_op jit(solution)/shard_map/ppermute | solution.py:261
  21.2 14.7 %collective-permute-start.6 = (bf16[512,256]{1,0:T(8,128)(2,1)S(1)}, bf16[512,256]{1,0:T(8,128)(2,1)S(1)}, u32[]{:S(2)}, u32[]{:S(2)}) collective-permute-start(bf16[512,256]{1,0:T(8,128)(2,1)S(1)} %fusion.40), channel_id=1, source_target_pairs={{0,1},{1,0},{2,3},{3,2},{4,5},{5,4},{6,7},{7,6},{8,9},{9,8},{10,11... | collective-permute-start | bytes 786440 | tf_op jit(solution)/shard_map/ppermute | solution.py:261
  21.4 26.0 %copy-start = (bf16[512,256]{1,0:T(8,128)(2,1)S(1)}, bf16[512,256]{1,0:T(8,128)(2,1)}, u32[]{:S(2)}) copy-start(bf16[512,256]{1,0:T(8,128)(2,1)} %refs_6_.1) | copy-start | bytes 786436
  21.4 25.9 %copy-start.1 = (bf16[256,256]{1,0:T(8,128)(2,1)S(1)}, bf16[256,256]{1,0:T(8,128)(2,1)}, u32[]{:S(2)}) copy-start(bf16[256,256]{1,0:T(8,128)(2,1)} %refs_4_.1) | copy-start | bytes 393220
  21.4 25.9 %copy-start.2 = (f32[256]{0:T(256)S(1)}, f32[256]{0:T(256)}, u32[]{:S(2)}) copy-start(f32[256]{0:T(256)} %param.18) | copy-start | bytes 3076
  21.5 8.6 %collective-permute-start.4 = (bf16[512,256]{1,0:T(8,128)(2,1)S(1)}, bf16[512,256]{1,0:T(8,128)(2,1)S(1)}, u32[]{:S(2)}, u32[]{:S(2)}) collective-permute-start(bf16[512,256]{1,0:T(8,128)(2,1)S(1)} %add_convert_fusion), channel_id=1, source_target_pairs={{0,2},{1,3},{2,0},{3,1},{4,6},{5,7},{6,4},{7,5},{8,10},{9,11},{10,... | collective-permute-start | bytes 786440 | tf_op jit(solution)/shard_map/ppermute | solution.py:261
  23.8 9.7 %collective-permute-start.7 = (bf16[512,256]{1,0:T(8,128)(2,1)S(1)}, bf16[512,256]{1,0:T(8,128)(2,1)S(1)}, u32[]{:S(2)}, u32[]{:S(2)}) collective-permute-start(bf16[512,256]{1,0:T(8,128)(2,1)S(1)} %fusion.43), channel_id=1, source_target_pairs={{0,1},{1,0},{2,3},{3,2},{4,5},{5,4},{6,7},{7,6},{8,9},{9,8},{10,11... | collective-permute-start | bytes 786440 | tf_op jit(solution)/shard_map/ppermute | solution.py:261
  24.0 12.6 %collective-permute-start.10 = (bf16[512,256]{1,0:T(8,128)(2,1)S(1)}, bf16[512,256]{1,0:T(8,128)(2,1)S(1)}, u32[]{:S(2)}, u32[]{:S(2)}) collective-permute-start(bf16[512,256]{1,0:T(8,128)(2,1)S(1)} %add_convert_fusion), channel_id=1, source_target_pairs={{2,4},{3,5},{4,2},{5,3},{10,12},{11,13},{12,10},{13,11},{18,20},{1... | collective-permute-start | bytes 786440 | tf_op jit(solution)/shard_map/ppermute | solution.py:266
  30.8 16.5 %collective-permute-start.9 = (bf16[512,256]{1,0:T(8,128)(2,1)S(1)}, bf16[512,256]{1,0:T(8,128)(2,1)S(1)}, u32[]{:S(2)}, u32[]{:S(2)}) collective-permute-start(bf16[512,256]{1,0:T(8,128)(2,1)S(1)} %fusion.31), channel_id=1, source_target_pairs={{0,4},{1,5},{2,6},{3,7},{4,0},{5,1},{6,2},{7,3},{8,12},{9,13},{10,... | collective-permute-start | bytes 786440 | tf_op jit(solution)/shard_map/ppermute | solution.py:261
  34.2 13.2 %collective-permute-start.8 = (bf16[512,256]{1,0:T(8,128)(2,1)S(1)}, bf16[512,256]{1,0:T(8,128)(2,1)S(1)}, u32[]{:S(2)}, u32[]{:S(2)}) collective-permute-start(bf16[512,256]{1,0:T(8,128)(2,1)S(1)} %fusion.28), channel_id=1, source_target_pairs={{0,2},{1,3},{2,0},{3,1},{4,6},{5,7},{6,4},{7,5},{8,10},{9,11},{10,... | collective-permute-start | bytes 786440 | tf_op jit(solution)/shard_map/ppermute | solution.py:261
  48.5 5.1 %collective-permute-start.15 = (bf16[272,256]{1,0:T(8,128)(2,1)S(1)}, bf16[272,256]{1,0:T(8,128)(2,1)S(1)}, u32[]{:S(2)}, u32[]{:S(2)}) collective-permute-start(bf16[272,256]{1,0:T(8,128)(2,1)S(1)} %get-tuple-element.81), channel_id=1, source_target_pairs={{0,8},{8,0},{16,24},{24,16},{1,9},{9,1},{17,25},{25,17},{2,10},{10... | collective-permute-start | bytes 417800 | tf_op jit(solution)/shard_map/ppermute | solution.py:261
  50.0 13.5 %collective-permute-start.14 = (bf16[256,512]{1,0:T(8,128)(2,1)S(1)}, bf16[256,512]{1,0:T(8,128)(2,1)S(1)}, u32[]{:S(2)}, u32[]{:S(2)}) collective-permute-start(bf16[256,512]{1,0:T(8,128)(2,1)S(1)} %get-tuple-element.80.refs_1_), channel_id=1, source_target_pairs={{0,4},{1,5},{2,6},{3,7},{4,0},{5,1},{6,2},{7,3},{8,12},{9,13},{10,... | collective-permute-start | bytes 786440 | tf_op jit(solution)/shard_map/ppermute | solution.py:261
  50.0 13.6 %collective-permute-start.12 = (bf16[256,512]{1,0:T(8,128)(2,1)S(1)}, bf16[256,512]{1,0:T(8,128)(2,1)S(1)}, u32[]{:S(2)}, u32[]{:S(2)}) collective-permute-start(bf16[256,512]{1,0:T(8,128)(2,1)S(1)} %get-tuple-element.80.refs_1_), channel_id=1, source_target_pairs={{0,2},{1,3},{2,0},{3,1},{4,6},{5,7},{6,4},{7,5},{8,10},{9,11},{10,... | collective-permute-start | bytes 786440 | tf_op jit(solution)/shard_map/ppermute | solution.py:261
  52.4 17.2 %collective-permute-start.18 = (bf16[256,512]{1,0:T(8,128)(2,1)S(1)}, bf16[256,512]{1,0:T(8,128)(2,1)S(1)}, u32[]{:S(2)}, u32[]{:S(2)}) collective-permute-start(bf16[256,512]{1,0:T(8,128)(2,1)S(1)} %get-tuple-element.80.refs_1_), channel_id=1, source_target_pairs={{2,4},{3,5},{4,2},{5,3},{10,12},{11,13},{12,10},{13,11},{18,20},{1... | collective-permute-start | bytes 786440 | tf_op jit(solution)/shard_map/ppermute | solution.py:266
  53.3 18.4 %collective-permute-start.11 = (bf16[256,512]{1,0:T(8,128)(2,1)S(1)}, bf16[256,512]{1,0:T(8,128)(2,1)S(1)}, u32[]{:S(2)}, u32[]{:S(2)}) collective-permute-start(bf16[256,512]{1,0:T(8,128)(2,1)S(1)} %get-tuple-element.80.refs_1_), channel_id=1, source_target_pairs={{0,1},{1,0},{2,3},{3,2},{4,5},{5,4},{6,7},{7,6},{8,9},{9,8},{10,11... | collective-permute-start | bytes 786440 | tf_op jit(solution)/shard_map/ppermute | solution.py:261
  63.5 8.1 %collective-permute-start.17 = (bf16[256,512]{1,0:T(8,128)(2,1)S(1)}, bf16[256,512]{1,0:T(8,128)(2,1)S(1)}, u32[]{:S(2)}, u32[]{:S(2)}) collective-permute-start(bf16[256,512]{1,0:T(8,128)(2,1)S(1)} %collective-permute-done.14.refs_3_), channel_id=1, source_target_pairs={{0,2},{1,3},{2,0},{3,1},{4,6},{5,7},{6,4},{7,5},{8,10},{9,11},{10,... | collective-permute-start | bytes 786440 | tf_op jit(solution)/shard_map/ppermute | solution.py:261
  63.5 8.3 %collective-permute-start.16 = (bf16[256,512]{1,0:T(8,128)(2,1)S(1)}, bf16[256,512]{1,0:T(8,128)(2,1)S(1)}, u32[]{:S(2)}, u32[]{:S(2)}) collective-permute-start(bf16[256,512]{1,0:T(8,128)(2,1)S(1)} %collective-permute-done.14.refs_3_), channel_id=1, source_target_pairs={{0,1},{1,0},{2,3},{3,2},{4,5},{5,4},{6,7},{7,6},{8,9},{9,8},{10,11... | collective-permute-start | bytes 786440 | tf_op jit(solution)/shard_map/ppermute | solution.py:261
  63.6 6.0 %collective-permute-start.22 = (bf16[272,256]{1,0:T(8,128)(2,1)S(1)}, bf16[272,256]{1,0:T(8,128)(2,1)S(1)}, u32[]{:S(2)}, u32[]{:S(2)}) collective-permute-start(bf16[272,256]{1,0:T(8,128)(2,1)S(1)} %add_convert_fusion.4), channel_id=1, source_target_pairs={{0,16},{8,24},{16,0},{24,8},{1,17},{9,25},{17,1},{25,9},{2,18},{10... | collective-permute-start | bytes 417800 | tf_op jit(solution)/shard_map/ppermute | solution.py:261
  69.5 2.2 %collective-permute-start.13 = (bf16[256,512]{1,0:T(8,128)(2,1)S(1)}, bf16[256,512]{1,0:T(8,128)(2,1)S(1)}, u32[]{:S(2)}, u32[]{:S(2)}) collective-permute-start(bf16[256,512]{1,0:T(8,128)(2,1)S(1)} %collective-permute-done.12.refs_2_), channel_id=1, source_target_pairs={{0,1},{1,0},{2,3},{3,2},{4,5},{5,4},{6,7},{7,6},{8,9},{9,8},{10,11... | collective-permute-start | bytes 786440 | tf_op jit(solution)/shard_map/ppermute | solution.py:261
  69.6 3.9 %collective-permute-start.23 = (bf16[272,256]{1,0:T(8,128)(2,1)S(1)}, bf16[272,256]{1,0:T(8,128)(2,1)S(1)}, u32[]{:S(2)}, u32[]{:S(2)}) collective-permute-start(bf16[272,256]{1,0:T(8,128)(2,1)S(1)} %add_convert_fusion.3), channel_id=1, source_target_pairs={{0,1},{1,0},{2,3},{3,2},{4,5},{5,4},{6,7},{7,6},{8,9},{9,8},{10,11... | collective-permute-start | bytes 417800 | tf_op jit(solution)/shard_map/ppermute | solution.py:261
  71.6 2.0 %collective-permute-start.19 = (bf16[256,512]{1,0:T(8,128)(2,1)S(1)}, bf16[256,512]{1,0:T(8,128)(2,1)S(1)}, u32[]{:S(2)}, u32[]{:S(2)}) collective-permute-start(bf16[256,512]{1,0:T(8,128)(2,1)S(1)} %broadcast_select_fusion.refs_1_), channel_id=1, source_target_pairs={{0,1},{1,0},{2,3},{3,2},{4,5},{5,4},{6,7},{7,6},{8,9},{9,8},{10,11... | collective-permute-start | bytes 786440 | tf_op jit(solution)/shard_map/ppermute | solution.py:261
  74.9 6.1 %collective-permute-start.25 = (bf16[272,256]{1,0:T(8,128)(2,1)S(1)}, bf16[272,256]{1,0:T(8,128)(2,1)S(1)}, u32[]{:S(2)}, u32[]{:S(2)}) collective-permute-start(bf16[272,256]{1,0:T(8,128)(2,1)S(1)} %add_convert_fusion.2), channel_id=1, source_target_pairs={{0,2},{1,3},{2,0},{3,1},{4,6},{5,7},{6,4},{7,5},{8,10},{9,11},{10,... | collective-permute-start | bytes 417800 | tf_op jit(solution)/shard_map/ppermute | solution.py:261
  76.3 10.1 %collective-permute-start.20 = (bf16[512,256]{1,0:T(8,128)(2,1)S(1)}, bf16[512,256]{1,0:T(8,128)(2,1)S(1)}, u32[]{:S(2)}, u32[]{:S(2)}) collective-permute-start(bf16[512,256]{1,0:T(8,128)(2,1)S(1)} %back_last.3), channel_id=1, source_target_pairs={{0,24},{8,16},{16,8},{24,0},{1,25},{9,17},{17,9},{25,1},{2,26},{10... | collective-permute-start | bytes 786440 | tf_op jit(solution)/shard_map/ppermute | solution.py:261
  77.8 12.6 %collective-permute-start.24 = (bf16[512,256]{1,0:T(8,128)(2,1)S(1)}, bf16[512,256]{1,0:T(8,128)(2,1)S(1)}, u32[]{:S(2)}, u32[]{:S(2)}) collective-permute-start(bf16[512,256]{1,0:T(8,128)(2,1)S(1)} %get-tuple-element.91), channel_id=1, source_target_pairs={{0,8},{8,0},{16,24},{24,16},{1,9},{9,1},{17,25},{25,17},{2,10},{10... | collective-permute-start | bytes 786440 | tf_op jit(solution)/shard_map/ppermute | solution.py:261
  78.7 12.2 %collective-permute-start.21 = (bf16[512,256]{1,0:T(8,128)(2,1)S(1)}, bf16[512,256]{1,0:T(8,128)(2,1)S(1)}, u32[]{:S(2)}, u32[]{:S(2)}) collective-permute-start(bf16[512,256]{1,0:T(8,128)(2,1)S(1)} %get-tuple-element.88), channel_id=1, source_target_pairs={{0,16},{8,24},{16,0},{24,8},{1,17},{9,25},{17,1},{25,9},{2,18},{10... | collective-permute-start | bytes 786440 | tf_op jit(solution)/shard_map/ppermute | solution.py:261
  81.1 10.0 %collective-permute-start.26 = (bf16[272,256]{1,0:T(8,128)(2,1)S(1)}, bf16[272,256]{1,0:T(8,128)(2,1)S(1)}, u32[]{:S(2)}, u32[]{:S(2)}) collective-permute-start(bf16[272,256]{1,0:T(8,128)(2,1)S(1)} %add_convert_fusion.1.refs_1_), channel_id=1, source_target_pairs={{0,4},{1,5},{2,6},{3,7},{4,0},{5,1},{6,2},{7,3},{8,12},{9,13},{10,... | collective-permute-start | bytes 417800 | tf_op jit(solution)/shard_map/ppermute | solution.py:261

commit v2 on v1

--- a/solution.py
+++ b/solution.py
@@ -348,8 +348,8 @@
     hidden, grad_agg, local = dense(own, parts, weight, bias, cotangent)
 
     first, *masks = doublings(1, row_count)
-    part = sum_over(local, "row", [first])
-    own_grads, part = gather_far(grad_agg, half, part)
+    own_grads, other = gather_far(grad_agg, half, swap(local, "row", first))
+    part = lax.optimization_barrier((local.astype(F32) + other.astype(F32)).astype(BF16))
     part = sum_over(part, "row", masks)
     part = sum_over(part, "col", [1])
     mate_grads = [swap(grads, "col", 1) for grads in own_grads[:far]]
@@ -360,11 +360,13 @@
         (total,) = back(list(range(half, half + far)), every, mate_grads, cell, total)
         panels = [far, half + far]
         grads = [own_grads[far], swap(own_grads[far], "col", 1)]
-        pieces = {}
-        rest = total
-        for chosen in ([row_count - 1], list(range(row_count - 2, 0, -1)), [0]):
-            pieces.update(zip(chosen, back(panels, chosen, grads, cell, rest, True)))
-            rest, pieces[chosen[-1]] = lax.optimization_barrier((total, pieces[chosen[-1]]))
+        outer, inner = row_count - 1, list(range(row_count - 2, 0, -1))
+        pieces = dict(zip([outer], back(panels, [outer], grads, cell, total, True)))
+        rest, part, pieces[outer] = lax.optimization_barrier((total, part, pieces[outer]))
+        landed = {outer: swap(pieces[outer], "row", outer)}
+        pieces.update(zip(inner, back(panels, inner, grads, cell, rest, True)))
+        rest, landed[outer] = lax.optimization_barrier((total, landed[outer]))
+        pieces.update(zip([0], back(panels, [0], grads, cell, rest, True)))
     else:
         own = jnp.concatenate(own_grads, axis=1)
         mate_grads.append(swap(own_grads[far], "col", 1))
@@ -375,12 +377,14 @@
             k: total[:, k * nodes : (k + 1) * nodes].T.astype(F32 if k == 0 else BF16)
             for k in range(row_count)
         }
-    part, pieces[1] = lax.optimization_barrier((part, pieces[1]))
-    landed = [swap(pieces[k], "row", k) for k in range(row_count - 1, 0, -1)]
+        landed = {}
+    for k in range(1, row_count):
+        if k not in landed:
+            landed[k] = swap(pieces[k], "row", k)
     *masks, mask = doublings(2, col_count)
     part = sum_over(part, "col", masks)
     value = pieces[0]
-    for piece in landed:
+    for piece in landed.values():
         value = value + piece.astype(F32)
     grad_features, grad_weight, grad_bias = finish(value, part, swap(part, "col", mask), factor)
     return (hidden, grad_weight, grad_bias[0], grad_features)

time: 92.1 us -> 90.5 us (0.983)
  starting transfers between devices: 24.4 us -> 22.8 us
    ppermute x25, starting transfers between devices: 22.9 us -> 21.3 us  [swap(): return lax.ppermute(value, axis, [(i, i ^ mask) for i in range(count)])]
  transfers between devices with their start and end apart: 27 -> 27, of which waited for: 14 -> 14; matrix products, arithmetic and copies ran while one was open for 6% -> 6% of each run, Pallas kernels for 12% -> 13%
where the time goes in v2:
time: 90.5 us; the launch traced here: 90.3 us
  waiting for transfers between devices  44.5 us (49%)
  starting transfers between devices  22.8 us (25%)
  Pallas kernels  14.3 us (16%)
  matrix products  5.67 us (6%)
  between operations  1.6 us (2%)
  local copies, waits for them, and re-layouts  1.09 us (1%)
    ppermute x25, waiting for transfers between devices, swap(): return lax.ppermute(value, axis, [(i, i ^ mask) for i in range(count)])  44.5 us
    ppermute x25, starting transfers between devices, swap(): return lax.ppermute(value, axis, [(i, i ^ mask) for i in range(count)])  21.3 us
    pallas_call x1, Pallas kernels, densify(): pl.pallas_call(lambda *refs: densify_kernel(per, col_count // 2, bands ==...  6.94 us
    dot_general x8, matrix products, cell_product(): return jnp.dot(cell_rows(core, k), source, preferred_element_type=F32)  5.67 us
    pallas_call x5, Pallas kernels, back(): pl.pallas_call(lambda *refs: back_kernel(panels, chosen, last, total is n...  5.43 us
  transfers between devices with their start and end apart: 27, of which 14 were waited for; matrix products, arithmetic and copies ran while one was open for 6% of the time, Pallas kernels for 13%

profile of v2, /device:TPU:0, one launch (start us, length us, event | category | flops | bytes accessed | tf_op | source)
XLA Modules:
  0.0 90.3 jit_solution(6694967825323121901)
XLA Ops:
  0.6 4.0 %collective-permute-start = (bf16[512,256]{1,0:T(8,128)(2,1)}, bf16[512,256]{1,0:T(8,128)(2,1)S(1)}, u32[]{:S(2)}, u32[]{:S(2)}) collective-permute-start(bf16[512,256]{1,0:T(8,128)(2,1)} %param.16), channel_id=1, source_target_pairs={{0,24},{8,16},{16,8},{24,0},{1,25},{9,17},{17,9},{25,1},{2,26},{10... | collective-permute-start | bytes 786440 | tf_op jit(solution)/shard_map/ppermute | solution.py:261
  4.6 0.5 collective-permute-start.1
  5.9 1.0 %scatter.14 = bf16[2048,256]{1,0:T(8,128)(2,1)S(1)} pad(bf16[512,256]{1,0:T(8,128)(2,1)} %param.16, bf16[]{:T(256)} %constant.127.clone.1), padding=0_1536x0_0 | pad | bytes 1310722 | tf_op jit(solution)/shard_map/scatter | solution.py:317
  6.9 6.9 %densify.1.refs_0_ = bf16[4096,2048]{1,0:T(8,128)(2,1)S(1)} custom-call(s32[1,1,384]{2,1,0:T(1,128)} %refs_0_.1, s32[1,1,384]{2,1,0:T(1,128)} %refs_1_.1, s32[1,1]{1,0:T(1,128)S(6)} %copy.15.refs_2_, bf16[384,128,128]{2,1,0:T(8,128)(2,1)} %bitcast.12, bf16[384,128,128]{2,1,0:T(8,128)(2,1)} %bitcast.13, bf16[384,128,128]{2,1,0:T(8,128)(2,1)} %bitcast.14), custom_call_target="tpu_custom_call" | custom-call | bytes 33554432 | tf_op jit(solution)/shard_map/densify/pallas_call | solution.py:93
  13.9 2.8 %collective-permute-done.1 = bf16[512,256]{1,0:T(8,128)(2,1)S(1)} collective-permute-done((bf16[512,256]{1,0:T(8,128)(2,1)}, bf16[512,256]{1,0:T(8,128)(2,1)S(1)}, u32[]{:S(2)}, u32[]{:S(2)}) %collective-permute-start.1) | collective-permute-done | bytes 262176 | tf_op jit(solution)/shard_map/ppermute | solution.py:261
  16.7 0.3 collective-permute-done.2
  17.0 0.7 fusion.37
  17.8 0.7 fusion.34
  18.5 0.5 collective-permute-start.5
  19.0 0.7 fusion.10
  19.8 0.7 collective-permute-done.5
  20.4 0.7 fusion.40
  21.5 1.7 %collective-permute-start.4 = (bf16[512,256]{1,0:T(8,128)(2,1)S(1)}, bf16[512,256]{1,0:T(8,128)(2,1)S(1)}, u32[]{:S(2)}, u32[]{:S(2)}) collective-permute-start(bf16[512,256]{1,0:T(8,128)(2,1)S(1)} %add_convert_fusion), channel_id=1, source_target_pairs={{0,2},{1,3},{2,0},{3,1},{4,6},{5,7},{6,4},{7,5},{8,10},{9,11},{10,... | collective-permute-start | bytes 786440 | tf_op jit(solution)/shard_map/ppermute | solution.py:261
  23.1 0.7 fusion.43
  24.0 0.7 collective-permute-start.10
  24.6 5.5 %collective-permute-done.4 = bf16[512,256]{1,0:T(8,128)(2,1)S(1)} collective-permute-done((bf16[512,256]{1,0:T(8,128)(2,1)S(1)}, bf16[512,256]{1,0:T(8,128)(2,1)S(1)}, u32[]{:S(2)}, u32[]{:S(2)}) %collective-permute-start.4) | collective-permute-done | bytes 262176 | tf_op jit(solution)/shard_map/ppermute | solution.py:261
  30.1 0.7 fusion.31
  30.8 2.9 %collective-permute-start.9 = (bf16[512,256]{1,0:T(8,128)(2,1)S(1)}, bf16[512,256]{1,0:T(8,128)(2,1)S(1)}, u32[]{:S(2)}, u32[]{:S(2)}) collective-permute-start(bf16[512,256]{1,0:T(8,128)(2,1)S(1)} %fusion.31), channel_id=1, source_target_pairs={{0,4},{1,5},{2,6},{3,7},{4,0},{5,1},{6,2},{7,3},{8,12},{9,13},{10,... | collective-permute-start | bytes 786440 | tf_op jit(solution)/shard_map/ppermute | solution.py:261
  33.8 0.7 fusion.28
  34.5 1.8 %collective-permute-start.8 = (bf16[512,256]{1,0:T(8,128)(2,1)S(1)}, bf16[512,256]{1,0:T(8,128)(2,1)S(1)}, u32[]{:S(2)}, u32[]{:S(2)}) collective-permute-start(bf16[512,256]{1,0:T(8,128)(2,1)S(1)} %fusion.28), channel_id=1, source_target_pairs={{0,2},{1,3},{2,0},{3,1},{4,6},{5,7},{6,4},{7,5},{8,10},{9,11},{10,... | collective-permute-start | bytes 786440 | tf_op jit(solution)/shard_map/ppermute | solution.py:261
  36.3 0.7 fusion.16.refs_0_
  37.0 10.9 %collective-permute-done.8.refs_1_ = bf16[512,256]{1,0:T(8,128)(2,1)S(1)} collective-permute-done((bf16[512,256]{1,0:T(8,128)(2,1)S(1)}, bf16[512,256]{1,0:T(8,128)(2,1)S(1)}, u32[]{:S(2)}, u32[]{:S(2)}) %collective-permute-start.8) | collective-permute-done | bytes 262176 | tf_op jit(solution)/shard_map/ppermute | solution.py:261
  47.9 1.1 %dense.1 = (bf16[512,256]{1,0:T(8,128)(2,1)}, bf16[256,512]{1,0:T(8,128)(2,1)S(1)}, bf16[272,256]{1,0:T(8,128)(2,1)S(1)}) custom-call(f32[512,256]{1,0:T(8,128)S(1)} %fusion.16.refs_0_, bf16[512,256]{1,0:T(8,128)(2,1)S(1)} %collective-permute-done.8.refs_1_, bf16[512,256]{1,0:T(8,128)(2,1)S(1)} %collective-permute-done.9.refs_2_, ...), custom_call_target="tpu_custom_call" | custom-call | flops 201326592 | bytes 1048576 | tf_op jit(solution)/shard_map/dense/pallas_call | solution.py:157
  49.0 1.0 %collective-permute-start.12 = (bf16[272,256]{1,0:T(8,128)(2,1)S(1)}, bf16[272,256]{1,0:T(8,128)(2,1)S(1)}, u32[]{:S(2)}, u32[]{:S(2)}) collective-permute-start(bf16[272,256]{1,0:T(8,128)(2,1)S(1)} %get-tuple-element.79), channel_id=1, source_target_pairs={{0,8},{8,0},{16,24},{24,16},{1,9},{9,1},{17,25},{25,17},{2,10},{10... | collective-permute-start | bytes 417800 | tf_op jit(solution)/shard_map/ppermute | solution.py:261
  50.0 2.4 %collective-permute-start.17 = (bf16[256,512]{1,0:T(8,128)(2,1)S(1)}, bf16[256,512]{1,0:T(8,128)(2,1)S(1)}, u32[]{:S(2)}, u32[]{:S(2)}) collective-permute-start(bf16[256,512]{1,0:T(8,128)(2,1)S(1)} %get-tuple-element.78.refs_1_), channel_id=1, source_target_pairs={{0,2},{1,3},{2,0},{3,1},{4,6},{5,7},{6,4},{7,5},{8,10},{9,11},{10,... | collective-permute-start | bytes 786440 | tf_op jit(solution)/shard_map/ppermute | solution.py:261
  52.4 0.8 collective-permute-start.14
  53.3 0.8 collective-permute-done.12
  54.0 8.7 %collective-permute-done.11.refs_3_ = bf16[256,512]{1,0:T(8,128)(2,1)S(1)} collective-permute-done((bf16[256,512]{1,0:T(8,128)(2,1)S(1)}, bf16[256,512]{1,0:T(8,128)(2,1)S(1)}, u32[]{:S(2)}, u32[]{:S(2)}) %collective-permute-start.11) | collective-permute-done | bytes 262176 | tf_op jit(solution)/shard_map/ppermute | solution.py:261
  62.8 0.7 collective-permute-done.17.refs_2_
  63.5 0.8 collective-permute-start.20
  64.3 1.8 %back.2.refs_4_ = f32[256,2048]{1,0:T(8,128)S(1)} custom-call(bf16[4096,2048]{1,0:T(8,128)(2,1)S(1)} %densify.1.refs_0_, bf16[256,512]{1,0:T(8,128)(2,1)S(1)} %get-tuple-element.78.refs_1_, bf16[256,512]{1,0:T(8,128)(2,1)S(1)} %collective-permute-done.17.refs_2_, bf16[256,512]{1,0:T(8,128)(2,1)S(1)} %collective-permute-done.11.refs_3_), custom_call_target="tpu_custom_call" | custom-call | flops 1610612736 | bytes 3145728 | tf_op jit(solution)/shard_map/back/pallas_call | solution.py:218
  66.1 2.9 %collective-permute-done.20 = bf16[272,256]{1,0:T(8,128)(2,1)S(1)} collective-permute-done((bf16[272,256]{1,0:T(8,128)(2,1)S(1)}, bf16[272,256]{1,0:T(8,128)(2,1)S(1)}, u32[]{:S(2)}, u32[]{:S(2)}) %collective-permute-start.20) | collective-permute-done | bytes 139296 | tf_op jit(solution)/shard_map/ppermute | solution.py:261
  69.0 0.6 collective-permute-start.21
  69.6 1.9 %collective-permute-done.13 = bf16[256,512]{1,0:T(8,128)(2,1)S(1)} collective-permute-done((bf16[256,512]{1,0:T(8,128)(2,1)S(1)}, bf16[256,512]{1,0:T(8,128)(2,1)S(1)}, u32[]{:S(2)}, u32[]{:S(2)}) %collective-permute-start.13) | collective-permute-done | bytes 262176 | tf_op jit(solution)/shard_map/ppermute | solution.py:261
  71.6 1.8 %back.3.refs_3_ = f32[256,2048]{1,0:T(8,128)S(1)} custom-call(bf16[4096,2048]{1,0:T(8,128)(2,1)S(1)} %densify.1.refs_0_, bf16[256,512]{1,0:T(8,128)(2,1)S(1)} %collective-permute-done.16.refs_1_, bf16[256,512]{1,0:T(8,128)(2,1)S(1)} %collective-permute-done.18.refs_2_, bf16[256,512]{1,0:T(8,128)(2,1)S(1)} %collective-permute-done.19.refs_3_, ...), custom_call_target="tpu_custom_call" | custom-call | flops 1610612736 | bytes 3145728 | tf_op jit(solution)/shard_map/back/pallas_call | solution.py:218
  73.5 0.5 back_last.3
  74.0 0.7 collective-permute-start.25
  74.7 1.2 %collective-permute-start.22 = (bf16[512,256]{1,0:T(8,128)(2,1)S(1)}, bf16[512,256]{1,0:T(8,128)(2,1)S(1)}, u32[]{:S(2)}, u32[]{:S(2)}) collective-permute-start(bf16[512,256]{1,0:T(8,128)(2,1)S(1)} %back_last.3), channel_id=1, source_target_pairs={{0,24},{8,16},{16,8},{24,0},{1,25},{9,17},{17,9},{25,1},{2,26},{10... | collective-permute-start | bytes 786440 | tf_op jit(solution)/shard_map/ppermute | solution.py:261
  75.9 0.8 back_last.5
  76.6 1.3 %collective-permute-start.23 = (bf16[512,256]{1,0:T(8,128)(2,1)S(1)}, bf16[512,256]{1,0:T(8,128)(2,1)S(1)}, u32[]{:S(2)}, u32[]{:S(2)}) collective-permute-start(bf16[512,256]{1,0:T(8,128)(2,1)S(1)} %get-tuple-element.86), channel_id=1, source_target_pairs={{0,8},{8,0},{16,24},{24,16},{1,9},{9,1},{17,25},{25,17},{2,10},{10... | collective-permute-start | bytes 786440 | tf_op jit(solution)/shard_map/ppermute | solution.py:261
  77.9 1.1 %collective-permute-start.24 = (bf16[512,256]{1,0:T(8,128)(2,1)S(1)}, bf16[512,256]{1,0:T(8,128)(2,1)S(1)}, u32[]{:S(2)}, u32[]{:S(2)}) collective-permute-start(bf16[512,256]{1,0:T(8,128)(2,1)S(1)} %get-tuple-element.87), channel_id=1, source_target_pairs={{0,16},{8,24},{16,0},{24,8},{1,17},{9,25},{17,1},{25,9},{2,18},{10... | collective-permute-start | bytes 786440 | tf_op jit(solution)/shard_map/ppermute | solution.py:261
  79.0 1.1 %collective-permute-done.25 = bf16[272,256]{1,0:T(8,128)(2,1)S(1)} collective-permute-done((bf16[272,256]{1,0:T(8,128)(2,1)S(1)}, bf16[272,256]{1,0:T(8,128)(2,1)S(1)}, u32[]{:S(2)}, u32[]{:S(2)}) %collective-permute-start.25) | collective-permute-done | bytes 139296 | tf_op jit(solution)/shard_map/ppermute | solution.py:261
  80.1 0.3 collective-permute-start.26
  80.4 4.4 %collective-permute-done.22 = bf16[512,256]{1,0:T(8,128)(2,1)S(1)} collective-permute-done((bf16[512,256]{1,0:T(8,128)(2,1)S(1)}, bf16[512,256]{1,0:T(8,128)(2,1)S(1)}, u32[]{:S(2)}, u32[]{:S(2)}) %collective-permute-start.22) | collective-permute-done | bytes 262176 | tf_op jit(solution)/shard_map/ppermute | solution.py:261
  84.8 0.6 back_last.4
  85.4 3.5 %collective-permute-done.23 = bf16[512,256]{1,0:T(8,128)(2,1)S(1)} collective-permute-done((bf16[512,256]{1,0:T(8,128)(2,1)S(1)}, bf16[512,256]{1,0:T(8,128)(2,1)S(1)}, u32[]{:S(2)}, u32[]{:S(2)}) %collective-permute-start.23) | collective-permute-done | bytes 262176 | tf_op jit(solution)/shard_map/ppermute | solution.py:261
  88.9 0.5 collective-permute-done.24
  89.4 0.8 finish.1
  (39 shorter events, 1.1 us)
Async XLA Ops:
  0.6 13.2 %collective-permute-start = (bf16[512,256]{1,0:T(8,128)(2,1)}, bf16[512,256]{1,0:T(8,128)(2,1)S(1)}, u32[]{:S(2)}, u32[]{:S(2)}) collective-permute-start(bf16[512,256]{1,0:T(8,128)(2,1)} %param.16), channel_id=1, source_target_pairs={{0,24},{8,16},{16,8},{24,0},{1,25},{9,17},{17,9},{25,1},{2,26},{10... | collective-permute-start | bytes 786440 | tf_op jit(solution)/shard_map/ppermute | solution.py:261
  4.6 12.1 %collective-permute-start.1 = (bf16[512,256]{1,0:T(8,128)(2,1)}, bf16[512,256]{1,0:T(8,128)(2,1)S(1)}, u32[]{:S(2)}, u32[]{:S(2)}) collective-permute-start(bf16[512,256]{1,0:T(8,128)(2,1)} %param.16), channel_id=1, source_target_pairs={{0,16},{8,24},{16,0},{24,8},{1,17},{9,25},{17,1},{25,9},{2,18},{10... | collective-permute-start | bytes 786440 | tf_op jit(solution)/shard_map/ppermute | solution.py:261
  5.1 11.9 %collective-permute-start.2 = (bf16[512,256]{1,0:T(8,128)(2,1)}, bf16[512,256]{1,0:T(8,128)(2,1)S(1)}, u32[]{:S(2)}, u32[]{:S(2)}) collective-permute-start(bf16[512,256]{1,0:T(8,128)(2,1)} %param.16), channel_id=1, source_target_pairs={{0,8},{8,0},{16,24},{24,16},{1,9},{9,1},{17,25},{25,17},{2,10},{10... | collective-permute-start | bytes 786440 | tf_op jit(solution)/shard_map/ppermute | solution.py:261
  18.5 2.9 %collective-permute-start.3 = (bf16[512,256]{1,0:T(8,128)(2,1)S(1)}, bf16[512,256]{1,0:T(8,128)(2,1)S(1)}, u32[]{:S(2)}, u32[]{:S(2)}) collective-permute-start(bf16[512,256]{1,0:T(8,128)(2,1)S(1)} %fusion.34), channel_id=1, source_target_pairs={{0,1},{1,0},{2,3},{3,2},{4,5},{5,4},{6,7},{7,6},{8,9},{9,8},{10,11... | collective-permute-start | bytes 786440 | tf_op jit(solution)/shard_map/ppermute | solution.py:261
  18.5 1.9 %collective-permute-start.5 = (bf16[512,256]{1,0:T(8,128)(2,1)S(1)}, bf16[512,256]{1,0:T(8,128)(2,1)S(1)}, u32[]{:S(2)}, u32[]{:S(2)}) collective-permute-start(bf16[512,256]{1,0:T(8,128)(2,1)S(1)} %fusion.37), channel_id=1, source_target_pairs={{0,1},{1,0},{2,3},{3,2},{4,5},{5,4},{6,7},{7,6},{8,9},{9,8},{10,11... | collective-permute-start | bytes 786440 | tf_op jit(solution)/shard_map/ppermute | solution.py:261
  21.2 15.1 %collective-permute-start.6 = (bf16[512,256]{1,0:T(8,128)(2,1)S(1)}, bf16[512,256]{1,0:T(8,128)(2,1)S(1)}, u32[]{:S(2)}, u32[]{:S(2)}) collective-permute-start(bf16[512,256]{1,0:T(8,128)(2,1)S(1)} %fusion.40), channel_id=1, source_target_pairs={{0,1},{1,0},{2,3},{3,2},{4,5},{5,4},{6,7},{7,6},{8,9},{9,8},{10,11... | collective-permute-start | bytes 786440 | tf_op jit(solution)/shard_map/ppermute | solution.py:261
  21.4 26.4 %copy-start = (bf16[512,256]{1,0:T(8,128)(2,1)S(1)}, bf16[512,256]{1,0:T(8,128)(2,1)}, u32[]{:S(2)}) copy-start(bf16[512,256]{1,0:T(8,128)(2,1)} %refs_6_.1) | copy-start | bytes 786436
  21.4 26.4 %copy-start.1 = (bf16[256,256]{1,0:T(8,128)(2,1)S(1)}, bf16[256,256]{1,0:T(8,128)(2,1)}, u32[]{:S(2)}) copy-start(bf16[256,256]{1,0:T(8,128)(2,1)} %refs_4_.1) | copy-start | bytes 393220
  21.4 26.4 %copy-start.2 = (f32[256]{0:T(256)S(1)}, f32[256]{0:T(256)}, u32[]{:S(2)}) copy-start(f32[256]{0:T(256)} %param.18) | copy-start | bytes 3076
  21.5 8.6 %collective-permute-start.4 = (bf16[512,256]{1,0:T(8,128)(2,1)S(1)}, bf16[512,256]{1,0:T(8,128)(2,1)S(1)}, u32[]{:S(2)}, u32[]{:S(2)}) collective-permute-start(bf16[512,256]{1,0:T(8,128)(2,1)S(1)} %add_convert_fusion), channel_id=1, source_target_pairs={{0,2},{1,3},{2,0},{3,1},{4,6},{5,7},{6,4},{7,5},{8,10},{9,11},{10,... | collective-permute-start | bytes 786440 | tf_op jit(solution)/shard_map/ppermute | solution.py:261
  23.8 9.9 %collective-permute-start.7 = (bf16[512,256]{1,0:T(8,128)(2,1)S(1)}, bf16[512,256]{1,0:T(8,128)(2,1)S(1)}, u32[]{:S(2)}, u32[]{:S(2)}) collective-permute-start(bf16[512,256]{1,0:T(8,128)(2,1)S(1)} %fusion.43), channel_id=1, source_target_pairs={{0,1},{1,0},{2,3},{3,2},{4,5},{5,4},{6,7},{7,6},{8,9},{9,8},{10,11... | collective-permute-start | bytes 786440 | tf_op jit(solution)/shard_map/ppermute | solution.py:261
  24.0 13.0 %collective-permute-start.10 = (bf16[512,256]{1,0:T(8,128)(2,1)S(1)}, bf16[512,256]{1,0:T(8,128)(2,1)S(1)}, u32[]{:S(2)}, u32[]{:S(2)}) collective-permute-start(bf16[512,256]{1,0:T(8,128)(2,1)S(1)} %add_convert_fusion), channel_id=1, source_target_pairs={{2,4},{3,5},{4,2},{5,3},{10,12},{11,13},{12,10},{13,11},{18,20},{1... | collective-permute-start | bytes 786440 | tf_op jit(solution)/shard_map/ppermute | solution.py:266
  30.8 17.0 %collective-permute-start.9 = (bf16[512,256]{1,0:T(8,128)(2,1)S(1)}, bf16[512,256]{1,0:T(8,128)(2,1)S(1)}, u32[]{:S(2)}, u32[]{:S(2)}) collective-permute-start(bf16[512,256]{1,0:T(8,128)(2,1)S(1)} %fusion.31), channel_id=1, source_target_pairs={{0,4},{1,5},{2,6},{3,7},{4,0},{5,1},{6,2},{7,3},{8,12},{9,13},{10,... | collective-permute-start | bytes 786440 | tf_op jit(solution)/shard_map/ppermute | solution.py:261
  34.5 13.4 %collective-permute-start.8 = (bf16[512,256]{1,0:T(8,128)(2,1)S(1)}, bf16[512,256]{1,0:T(8,128)(2,1)S(1)}, u32[]{:S(2)}, u32[]{:S(2)}) collective-permute-start(bf16[512,256]{1,0:T(8,128)(2,1)S(1)} %fusion.28), channel_id=1, source_target_pairs={{0,2},{1,3},{2,0},{3,1},{4,6},{5,7},{6,4},{7,5},{8,10},{9,11},{10,... | collective-permute-start | bytes 786440 | tf_op jit(solution)/shard_map/ppermute | solution.py:261
  49.0 13.7 %collective-permute-start.11 = (bf16[256,512]{1,0:T(8,128)(2,1)S(1)}, bf16[256,512]{1,0:T(8,128)(2,1)S(1)}, u32[]{:S(2)}, u32[]{:S(2)}) collective-permute-start(bf16[256,512]{1,0:T(8,128)(2,1)S(1)} %get-tuple-element.78.refs_1_), channel_id=1, source_target_pairs={{0,4},{1,5},{2,6},{3,7},{4,0},{5,1},{6,2},{7,3},{8,12},{9,13},{10,... | collective-permute-start | bytes 786440 | tf_op jit(solution)/shard_map/ppermute | solution.py:261
  49.0 5.1 %collective-permute-start.12 = (bf16[272,256]{1,0:T(8,128)(2,1)S(1)}, bf16[272,256]{1,0:T(8,128)(2,1)S(1)}, u32[]{:S(2)}, u32[]{:S(2)}) collective-permute-start(bf16[272,256]{1,0:T(8,128)(2,1)S(1)} %get-tuple-element.79), channel_id=1, source_target_pairs={{0,8},{8,0},{16,24},{24,16},{1,9},{9,1},{17,25},{25,17},{2,10},{10... | collective-permute-start | bytes 417800 | tf_op jit(solution)/shard_map/ppermute | solution.py:261
  50.0 13.5 %collective-permute-start.17 = (bf16[256,512]{1,0:T(8,128)(2,1)S(1)}, bf16[256,512]{1,0:T(8,128)(2,1)S(1)}, u32[]{:S(2)}, u32[]{:S(2)}) collective-permute-start(bf16[256,512]{1,0:T(8,128)(2,1)S(1)} %get-tuple-element.78.refs_1_), channel_id=1, source_target_pairs={{0,2},{1,3},{2,0},{3,1},{4,6},{5,7},{6,4},{7,5},{8,10},{9,11},{10,... | collective-permute-start | bytes 786440 | tf_op jit(solution)/shard_map/ppermute | solution.py:261
  52.4 19.2 %collective-permute-start.16 = (bf16[256,512]{1,0:T(8,128)(2,1)S(1)}, bf16[256,512]{1,0:T(8,128)(2,1)S(1)}, u32[]{:S(2)}, u32[]{:S(2)}) collective-permute-start(bf16[256,512]{1,0:T(8,128)(2,1)S(1)} %get-tuple-element.78.refs_1_), channel_id=1, source_target_pairs={{0,1},{1,0},{2,3},{3,2},{4,5},{5,4},{6,7},{7,6},{8,9},{9,8},{10,11... | collective-permute-start | bytes 786440 | tf_op jit(solution)/shard_map/ppermute | solution.py:261
  52.4 16.6 %collective-permute-start.14 = (bf16[256,512]{1,0:T(8,128)(2,1)S(1)}, bf16[256,512]{1,0:T(8,128)(2,1)S(1)}, u32[]{:S(2)}, u32[]{:S(2)}) collective-permute-start(bf16[256,512]{1,0:T(8,128)(2,1)S(1)} %get-tuple-element.78.refs_1_), channel_id=1, source_target_pairs={{2,4},{3,5},{4,2},{5,3},{10,12},{11,13},{12,10},{13,11},{18,20},{1... | collective-permute-start | bytes 786440 | tf_op jit(solution)/shard_map/ppermute | solution.py:266
  62.7 8.9 %collective-permute-start.19 = (bf16[256,512]{1,0:T(8,128)(2,1)S(1)}, bf16[256,512]{1,0:T(8,128)(2,1)S(1)}, u32[]{:S(2)}, u32[]{:S(2)}) collective-permute-start(bf16[256,512]{1,0:T(8,128)(2,1)S(1)} %collective-permute-done.11.refs_3_), channel_id=1, source_target_pairs={{0,1},{1,0},{2,3},{3,2},{4,5},{5,4},{6,7},{7,6},{8,9},{9,8},{10,11... | collective-permute-start | bytes 786440 | tf_op jit(solution)/shard_map/ppermute | solution.py:261
  62.7 8.7 %collective-permute-start.13 = (bf16[256,512]{1,0:T(8,128)(2,1)S(1)}, bf16[256,512]{1,0:T(8,128)(2,1)S(1)}, u32[]{:S(2)}, u32[]{:S(2)}) collective-permute-start(bf16[256,512]{1,0:T(8,128)(2,1)S(1)} %collective-permute-done.11.refs_3_), channel_id=1, source_target_pairs={{0,2},{1,3},{2,0},{3,1},{4,6},{5,7},{6,4},{7,5},{8,10},{9,11},{10,... | collective-permute-start | bytes 786440 | tf_op jit(solution)/shard_map/ppermute | solution.py:261
  63.5 5.4 %collective-permute-start.20 = (bf16[272,256]{1,0:T(8,128)(2,1)S(1)}, bf16[272,256]{1,0:T(8,128)(2,1)S(1)}, u32[]{:S(2)}, u32[]{:S(2)}) collective-permute-start(bf16[272,256]{1,0:T(8,128)(2,1)S(1)} %add_convert_fusion.4), channel_id=1, source_target_pairs={{0,16},{8,24},{16,0},{24,8},{1,17},{9,25},{17,1},{25,9},{2,18},{10... | collective-permute-start | bytes 417800 | tf_op jit(solution)/shard_map/ppermute | solution.py:261
  68.9 2.6 %collective-permute-start.18 = (bf16[256,512]{1,0:T(8,128)(2,1)S(1)}, bf16[256,512]{1,0:T(8,128)(2,1)S(1)}, u32[]{:S(2)}, u32[]{:S(2)}) collective-permute-start(bf16[256,512]{1,0:T(8,128)(2,1)S(1)} %collective-permute-done.17.refs_2_), channel_id=1, source_target_pairs={{0,1},{1,0},{2,3},{3,2},{4,5},{5,4},{6,7},{7,6},{8,9},{9,8},{10,11... | collective-permute-start | bytes 786440 | tf_op jit(solution)/shard_map/ppermute | solution.py:261
  69.0 4.4 %collective-permute-start.21 = (bf16[272,256]{1,0:T(8,128)(2,1)S(1)}, bf16[272,256]{1,0:T(8,128)(2,1)S(1)}, u32[]{:S(2)}, u32[]{:S(2)}) collective-permute-start(bf16[272,256]{1,0:T(8,128)(2,1)S(1)} %add_convert_fusion.3), channel_id=1, source_target_pairs={{0,1},{1,0},{2,3},{3,2},{4,5},{5,4},{6,7},{7,6},{8,9},{9,8},{10,11... | collective-permute-start | bytes 417800 | tf_op jit(solution)/shard_map/ppermute | solution.py:261
  71.5 2.0 %collective-permute-start.15 = (bf16[256,512]{1,0:T(8,128)(2,1)S(1)}, bf16[256,512]{1,0:T(8,128)(2,1)S(1)}, u32[]{:S(2)}, u32[]{:S(2)}) collective-permute-start(bf16[256,512]{1,0:T(8,128)(2,1)S(1)} %broadcast_select_fusion.refs_1_), channel_id=1, source_target_pairs={{0,1},{1,0},{2,3},{3,2},{4,5},{5,4},{6,7},{7,6},{8,9},{9,8},{10,11... | collective-permute-start | bytes 786440 | tf_op jit(solution)/shard_map/ppermute | solution.py:261
  74.0 6.1 %collective-permute-start.25 = (bf16[272,256]{1,0:T(8,128)(2,1)S(1)}, bf16[272,256]{1,0:T(8,128)(2,1)S(1)}, u32[]{:S(2)}, u32[]{:S(2)}) collective-permute-start(bf16[272,256]{1,0:T(8,128)(2,1)S(1)} %add_convert_fusion.2), channel_id=1, source_target_pairs={{0,2},{1,3},{2,0},{3,1},{4,6},{5,7},{6,4},{7,5},{8,10},{9,11},{10,... | collective-permute-start | bytes 417800 | tf_op jit(solution)/shard_map/ppermute | solution.py:261
  74.7 10.1 %collective-permute-start.22 = (bf16[512,256]{1,0:T(8,128)(2,1)S(1)}, bf16[512,256]{1,0:T(8,128)(2,1)S(1)}, u32[]{:S(2)}, u32[]{:S(2)}) collective-permute-start(bf16[512,256]{1,0:T(8,128)(2,1)S(1)} %back_last.3), channel_id=1, source_target_pairs={{0,24},{8,16},{16,8},{24,0},{1,25},{9,17},{17,9},{25,1},{2,26},{10... | collective-permute-start | bytes 786440 | tf_op jit(solution)/shard_map/ppermute | solution.py:261
  76.6 12.2 %collective-permute-start.23 = (bf16[512,256]{1,0:T(8,128)(2,1)S(1)}, bf16[512,256]{1,0:T(8,128)(2,1)S(1)}, u32[]{:S(2)}, u32[]{:S(2)}) collective-permute-start(bf16[512,256]{1,0:T(8,128)(2,1)S(1)} %get-tuple-element.86), channel_id=1, source_target_pairs={{0,8},{8,0},{16,24},{24,16},{1,9},{9,1},{17,25},{25,17},{2,10},{10... | collective-permute-start | bytes 786440 | tf_op jit(solution)/shard_map/ppermute | solution.py:261
  77.9 11.4 %collective-permute-start.24 = (bf16[512,256]{1,0:T(8,128)(2,1)S(1)}, bf16[512,256]{1,0:T(8,128)(2,1)S(1)}, u32[]{:S(2)}, u32[]{:S(2)}) collective-permute-start(bf16[512,256]{1,0:T(8,128)(2,1)S(1)} %get-tuple-element.87), channel_id=1, source_target_pairs={{0,16},{8,24},{16,0},{24,8},{1,17},{9,25},{17,1},{25,9},{2,18},{10... | collective-permute-start | bytes 786440 | tf_op jit(solution)/shard_map/ppermute | solution.py:261
  80.1 9.3 %collective-permute-start.26 = (bf16[272,256]{1,0:T(8,128)(2,1)S(1)}, bf16[272,256]{1,0:T(8,128)(2,1)S(1)}, u32[]{:S(2)}, u32[]{:S(2)}) collective-permute-start(bf16[272,256]{1,0:T(8,128)(2,1)S(1)} %add_convert_fusion.1.refs_1_), channel_id=1, source_target_pairs={{0,4},{1,5},{2,6},{3,7},{4,0},{5,1},{6,2},{7,3},{8,12},{9,13},{10,... | collective-permute-start | bytes 417800 | tf_op jit(solution)/shard_map/ppermute | solution.py:261

commit v3 on v2

--- a/solution.py
+++ b/solution.py
@@ -283,10 +283,11 @@
 def gather_far(value, count, hold):
     if count != 4:
         return [value] + [swap(value, "col", 2 * k) for k in range(1, count)], hold
+    later, hold = lax.optimization_barrier((value, hold))
     across, hold = lax.optimization_barrier((swap(value, "col", 4), hold))
     near = swap(value, "col", 2)
     passed = swap(across, "col", 2)
-    middle = move(value, [(1, 2), (2, 1)])
+    middle = move(later, [(1, 2), (2, 1)])
     return [value, near, across, jnp.where(at_end(), passed, middle)], hold
 
 

time: 90.5 us -> 90.5 us (level)
  waiting for transfers between devices: 44.5 us -> 42.8 us
  Pallas kernels: 14.3 us -> 16 us
    ppermute x25, waiting for transfers between devices: 44.5 us -> 42.8 us  [swap(): return lax.ppermute(value, axis, [(i, i ^ mask) for i in range(count)])]
    pallas_call x1, Pallas kernels: 6.94 us -> 8.61 us  [densify(): pl.pallas_call(lambda *refs: densify_kernel(per, col_count // 2, bands ==...]
  transfers between devices with their start and end apart: 27 -> 27, of which waited for: 14 -> 14; matrix products, arithmetic and copies ran while one was open for 6% -> 6% of each run, Pallas kernels for 13% -> 15%
where the time goes in v3:
time: 90.5 us; the launch traced here: 90.3 us
  waiting for transfers between devices  42.8 us (47%)
  starting transfers between devices  22.8 us (25%)
  Pallas kernels  16 us (18%)
  matrix products  5.67 us (6%)
  between operations  1.6 us (2%)
  local copies, waits for them, and re-layouts  1.09 us (1%)
    ppermute x25, waiting for transfers between devices, swap(): return lax.ppermute(value, axis, [(i, i ^ mask) for i in range(count)])  42.8 us
    ppermute x25, starting transfers between devices, swap(): return lax.ppermute(value, axis, [(i, i ^ mask) for i in range(count)])  21.3 us
    pallas_call x1, Pallas kernels, densify(): pl.pallas_call(lambda *refs: densify_kernel(per, col_count // 2, bands ==...  8.61 us
    dot_general x8, matrix products, cell_product(): return jnp.dot(cell_rows(core, k), source, preferred_element_type=F32)  5.67 us
    pallas_call x5, Pallas kernels, back(): pl.pallas_call(lambda *refs: back_kernel(panels, chosen, last, total is n...  5.43 us
  transfers between devices with their start and end apart: 27, of which 14 were waited for; matrix products, arithmetic and copies ran while one was open for 6% of the time, Pallas kernels for 15%

profile of v3, /device:TPU:0, one launch (start us, length us, event | category | flops | bytes accessed | tf_op | source)
XLA Modules:
  0.0 90.3 jit_solution(16709280717943458706)
XLA Ops:
  0.6 4.0 %collective-permute-start = (bf16[512,256]{1,0:T(8,128)(2,1)}, bf16[512,256]{1,0:T(8,128)(2,1)S(1)}, u32[]{:S(2)}, u32[]{:S(2)}) collective-permute-start(bf16[512,256]{1,0:T(8,128)(2,1)} %param.16), channel_id=1, source_target_pairs={{0,24},{8,16},{16,8},{24,0},{1,25},{9,17},{17,9},{25,1},{2,26},{10... | collective-permute-start | bytes 786440 | tf_op jit(solution)/shard_map/ppermute | solution.py:261
  4.6 0.5 collective-permute-start.1
  5.9 1.0 %scatter.14 = bf16[2048,256]{1,0:T(8,128)(2,1)S(1)} pad(bf16[512,256]{1,0:T(8,128)(2,1)} %param.16, bf16[]{:T(256)} %constant.127.clone.1), padding=0_1536x0_0 | pad | bytes 1310722 | tf_op jit(solution)/shard_map/scatter | solution.py:318
  6.9 8.6 %densify.1.refs_0_ = bf16[4096,2048]{1,0:T(8,128)(2,1)S(1)} custom-call(s32[1,1,384]{2,1,0:T(1,128)} %refs_0_.1, s32[1,1,384]{2,1,0:T(1,128)} %refs_1_.1, s32[1,1]{1,0:T(1,128)S(6)} %copy.15.refs_2_, bf16[384,128,128]{2,1,0:T(8,128)(2,1)} %bitcast.12, bf16[384,128,128]{2,1,0:T(8,128)(2,1)} %bitcast.13, bf16[384,128,128]{2,1,0:T(8,128)(2,1)} %bitcast.14), custom_call_target="tpu_custom_call" | custom-call | bytes 33554432 | tf_op jit(solution)/shard_map/densify/pallas_call | solution.py:93
  15.6 1.2 %collective-permute-done.1 = bf16[512,256]{1,0:T(8,128)(2,1)S(1)} collective-permute-done((bf16[512,256]{1,0:T(8,128)(2,1)}, bf16[512,256]{1,0:T(8,128)(2,1)S(1)}, u32[]{:S(2)}, u32[]{:S(2)}) %collective-permute-start.1) | collective-permute-done | bytes 262176 | tf_op jit(solution)/shard_map/ppermute | solution.py:261
  16.7 0.3 collective-permute-done.2
  17.0 0.7 fusion.37
  17.8 0.7 fusion.34
  18.5 0.5 collective-permute-start.5
  19.0 0.7 fusion.10
  19.8 0.7 collective-permute-done.5
  20.4 0.7 fusion.40
  21.5 1.7 %collective-permute-start.4 = (bf16[512,256]{1,0:T(8,128)(2,1)S(1)}, bf16[512,256]{1,0:T(8,128)(2,1)S(1)}, u32[]{:S(2)}, u32[]{:S(2)}) collective-permute-start(bf16[512,256]{1,0:T(8,128)(2,1)S(1)} %add_convert_fusion), channel_id=1, source_target_pairs={{0,2},{1,3},{2,0},{3,1},{4,6},{5,7},{6,4},{7,5},{8,10},{9,11},{10,... | collective-permute-start | bytes 786440 | tf_op jit(solution)/shard_map/ppermute | solution.py:261
  23.1 0.7 fusion.43
  24.0 0.7 collective-permute-start.10
  24.6 5.5 %collective-permute-done.4 = bf16[512,256]{1,0:T(8,128)(2,1)S(1)} collective-permute-done((bf16[512,256]{1,0:T(8,128)(2,1)S(1)}, bf16[512,256]{1,0:T(8,128)(2,1)S(1)}, u32[]{:S(2)}, u32[]{:S(2)}) %collective-permute-start.4) | collective-permute-done | bytes 262176 | tf_op jit(solution)/shard_map/ppermute | solution.py:261
  30.1 0.7 fusion.31
  30.8 2.9 %collective-permute-start.9 = (bf16[512,256]{1,0:T(8,128)(2,1)S(1)}, bf16[512,256]{1,0:T(8,128)(2,1)S(1)}, u32[]{:S(2)}, u32[]{:S(2)}) collective-permute-start(bf16[512,256]{1,0:T(8,128)(2,1)S(1)} %fusion.31), channel_id=1, source_target_pairs={{0,4},{1,5},{2,6},{3,7},{4,0},{5,1},{6,2},{7,3},{8,12},{9,13},{10,... | collective-permute-start | bytes 786440 | tf_op jit(solution)/shard_map/ppermute | solution.py:261
  33.8 0.7 fusion.28
  34.5 1.8 %collective-permute-start.8 = (bf16[512,256]{1,0:T(8,128)(2,1)S(1)}, bf16[512,256]{1,0:T(8,128)(2,1)S(1)}, u32[]{:S(2)}, u32[]{:S(2)}) collective-permute-start(bf16[512,256]{1,0:T(8,128)(2,1)S(1)} %fusion.28), channel_id=1, source_target_pairs={{0,2},{1,3},{2,0},{3,1},{4,6},{5,7},{6,4},{7,5},{8,10},{9,11},{10,... | collective-permute-start | bytes 786440 | tf_op jit(solution)/shard_map/ppermute | solution.py:261
  36.3 0.7 fusion.16.refs_0_
  37.0 10.9 %collective-permute-done.8.refs_1_ = bf16[512,256]{1,0:T(8,128)(2,1)S(1)} collective-permute-done((bf16[512,256]{1,0:T(8,128)(2,1)S(1)}, bf16[512,256]{1,0:T(8,128)(2,1)S(1)}, u32[]{:S(2)}, u32[]{:S(2)}) %collective-permute-start.8) | collective-permute-done | bytes 262176 | tf_op jit(solution)/shard_map/ppermute | solution.py:261
  47.9 1.1 %dense.1 = (bf16[512,256]{1,0:T(8,128)(2,1)}, bf16[256,512]{1,0:T(8,128)(2,1)S(1)}, bf16[272,256]{1,0:T(8,128)(2,1)S(1)}) custom-call(f32[512,256]{1,0:T(8,128)S(1)} %fusion.16.refs_0_, bf16[512,256]{1,0:T(8,128)(2,1)S(1)} %collective-permute-done.8.refs_1_, bf16[512,256]{1,0:T(8,128)(2,1)S(1)} %collective-permute-done.9.refs_2_, ...), custom_call_target="tpu_custom_call" | custom-call | flops 201326592 | bytes 1048576 | tf_op jit(solution)/shard_map/dense/pallas_call | solution.py:157
  49.0 1.0 %collective-permute-start.12 = (bf16[272,256]{1,0:T(8,128)(2,1)S(1)}, bf16[272,256]{1,0:T(8,128)(2,1)S(1)}, u32[]{:S(2)}, u32[]{:S(2)}) collective-permute-start(bf16[272,256]{1,0:T(8,128)(2,1)S(1)} %get-tuple-element.81), channel_id=1, source_target_pairs={{0,8},{8,0},{16,24},{24,16},{1,9},{9,1},{17,25},{25,17},{2,10},{10... | collective-permute-start | bytes 417800 | tf_op jit(solution)/shard_map/ppermute | solution.py:261
  50.0 2.4 %collective-permute-start.17 = (bf16[256,512]{1,0:T(8,128)(2,1)S(1)}, bf16[256,512]{1,0:T(8,128)(2,1)S(1)}, u32[]{:S(2)}, u32[]{:S(2)}) collective-permute-start(bf16[256,512]{1,0:T(8,128)(2,1)S(1)} %get-tuple-element.84.refs_1_), channel_id=1, source_target_pairs={{0,2},{1,3},{2,0},{3,1},{4,6},{5,7},{6,4},{7,5},{8,10},{9,11},{10,... | collective-permute-start | bytes 786440 | tf_op jit(solution)/shard_map/ppermute | solution.py:261
  52.4 1.6 %collective-permute-done.12 = bf16[272,256]{1,0:T(8,128)(2,1)S(1)} collective-permute-done((bf16[272,256]{1,0:T(8,128)(2,1)S(1)}, bf16[272,256]{1,0:T(8,128)(2,1)S(1)}, u32[]{:S(2)}, u32[]{:S(2)}) %collective-permute-start.12) | collective-permute-done | bytes 139296 | tf_op jit(solution)/shard_map/ppermute | solution.py:261
  54.0 0.8 collective-permute-start.14
  54.9 7.8 %collective-permute-done.11.refs_3_ = bf16[256,512]{1,0:T(8,128)(2,1)S(1)} collective-permute-done((bf16[256,512]{1,0:T(8,128)(2,1)S(1)}, bf16[256,512]{1,0:T(8,128)(2,1)S(1)}, u32[]{:S(2)}, u32[]{:S(2)}) %collective-permute-start.11) | collective-permute-done | bytes 262176 | tf_op jit(solution)/shard_map/ppermute | solution.py:261
  62.8 0.7 collective-permute-done.17.refs_2_
  63.5 0.8 collective-permute-start.20
  64.3 1.8 %back.2.refs_4_ = f32[256,2048]{1,0:T(8,128)S(1)} custom-call(bf16[4096,2048]{1,0:T(8,128)(2,1)S(1)} %densify.1.refs_0_, bf16[256,512]{1,0:T(8,128)(2,1)S(1)} %get-tuple-element.84.refs_1_, bf16[256,512]{1,0:T(8,128)(2,1)S(1)} %collective-permute-done.17.refs_2_, bf16[256,512]{1,0:T(8,128)(2,1)S(1)} %collective-permute-done.11.refs_3_), custom_call_target="tpu_custom_call" | custom-call | flops 1610612736 | bytes 3145728 | tf_op jit(solution)/shard_map/back/pallas_call | solution.py:218
  66.1 2.9 %collective-permute-done.20 = bf16[272,256]{1,0:T(8,128)(2,1)S(1)} collective-permute-done((bf16[272,256]{1,0:T(8,128)(2,1)S(1)}, bf16[272,256]{1,0:T(8,128)(2,1)S(1)}, u32[]{:S(2)}, u32[]{:S(2)}) %collective-permute-start.20) | collective-permute-done | bytes 139296 | tf_op jit(solution)/shard_map/ppermute | solution.py:261
  69.0 0.6 collective-permute-start.21
  69.6 1.9 %collective-permute-done.13 = bf16[256,512]{1,0:T(8,128)(2,1)S(1)} collective-permute-done((bf16[256,512]{1,0:T(8,128)(2,1)S(1)}, bf16[256,512]{1,0:T(8,128)(2,1)S(1)}, u32[]{:S(2)}, u32[]{:S(2)}) %collective-permute-start.13) | collective-permute-done | bytes 262176 | tf_op jit(solution)/shard_map/ppermute | solution.py:261
  71.6 1.8 %back.3.refs_3_ = f32[256,2048]{1,0:T(8,128)S(1)} custom-call(bf16[4096,2048]{1,0:T(8,128)(2,1)S(1)} %densify.1.refs_0_, bf16[256,512]{1,0:T(8,128)(2,1)S(1)} %collective-permute-done.16.refs_1_, bf16[256,512]{1,0:T(8,128)(2,1)S(1)} %collective-permute-done.18.refs_2_, bf16[256,512]{1,0:T(8,128)(2,1)S(1)} %collective-permute-done.19.refs_3_, ...), custom_call_target="tpu_custom_call" | custom-call | flops 1610612736 | bytes 3145728 | tf_op jit(solution)/shard_map/back/pallas_call | solution.py:218
  73.5 0.5 back_last.3
  74.0 0.7 collective-permute-start.25
  74.7 1.2 %collective-permute-start.22 = (bf16[512,256]{1,0:T(8,128)(2,1)S(1)}, bf16[512,256]{1,0:T(8,128)(2,1)S(1)}, u32[]{:S(2)}, u32[]{:S(2)}) collective-permute-start(bf16[512,256]{1,0:T(8,128)(2,1)S(1)} %back_last.3), channel_id=1, source_target_pairs={{0,24},{8,16},{16,8},{24,0},{1,25},{9,17},{17,9},{25,1},{2,26},{10... | collective-permute-start | bytes 786440 | tf_op jit(solution)/shard_map/ppermute | solution.py:261
  75.9 0.8 back_last.5
  76.6 1.3 %collective-permute-start.23 = (bf16[512,256]{1,0:T(8,128)(2,1)S(1)}, bf16[512,256]{1,0:T(8,128)(2,1)S(1)}, u32[]{:S(2)}, u32[]{:S(2)}) collective-permute-start(bf16[512,256]{1,0:T(8,128)(2,1)S(1)} %get-tuple-element.90), channel_id=1, source_target_pairs={{0,8},{8,0},{16,24},{24,16},{1,9},{9,1},{17,25},{25,17},{2,10},{10... | collective-permute-start | bytes 786440 | tf_op jit(solution)/shard_map/ppermute | solution.py:261
  77.9 1.1 %collective-permute-start.24 = (bf16[512,256]{1,0:T(8,128)(2,1)S(1)}, bf16[512,256]{1,0:T(8,128)(2,1)S(1)}, u32[]{:S(2)}, u32[]{:S(2)}) collective-permute-start(bf16[512,256]{1,0:T(8,128)(2,1)S(1)} %get-tuple-element.91), channel_id=1, source_target_pairs={{0,16},{8,24},{16,0},{24,8},{1,17},{9,25},{17,1},{25,9},{2,18},{10... | collective-permute-start | bytes 786440 | tf_op jit(solution)/shard_map/ppermute | solution.py:261
  79.0 1.1 %collective-permute-done.25 = bf16[272,256]{1,0:T(8,128)(2,1)S(1)} collective-permute-done((bf16[272,256]{1,0:T(8,128)(2,1)S(1)}, bf16[272,256]{1,0:T(8,128)(2,1)S(1)}, u32[]{:S(2)}, u32[]{:S(2)}) %collective-permute-start.25) | collective-permute-done | bytes 139296 | tf_op jit(solution)/shard_map/ppermute | solution.py:261
  80.1 0.3 collective-permute-start.26
  80.4 4.4 %collective-permute-done.22 = bf16[512,256]{1,0:T(8,128)(2,1)S(1)} collective-permute-done((bf16[512,256]{1,0:T(8,128)(2,1)S(1)}, bf16[512,256]{1,0:T(8,128)(2,1)S(1)}, u32[]{:S(2)}, u32[]{:S(2)}) %collective-permute-start.22) | collective-permute-done | bytes 262176 | tf_op jit(solution)/shard_map/ppermute | solution.py:261
  84.8 0.6 back_last.4
  85.4 3.5 %collective-permute-done.23 = bf16[512,256]{1,0:T(8,128)(2,1)S(1)} collective-permute-done((bf16[512,256]{1,0:T(8,128)(2,1)S(1)}, bf16[512,256]{1,0:T(8,128)(2,1)S(1)}, u32[]{:S(2)}, u32[]{:S(2)}) %collective-permute-start.23) | collective-permute-done | bytes 262176 | tf_op jit(solution)/shard_map/ppermute | solution.py:261
  88.9 0.5 collective-permute-done.24
  89.4 0.8 finish.1
  (39 shorter events, 1.1 us)
Async XLA Ops:
  0.6 14.9 %collective-permute-start = (bf16[512,256]{1,0:T(8,128)(2,1)}, bf16[512,256]{1,0:T(8,128)(2,1)S(1)}, u32[]{:S(2)}, u32[]{:S(2)}) collective-permute-start(bf16[512,256]{1,0:T(8,128)(2,1)} %param.16), channel_id=1, source_target_pairs={{0,24},{8,16},{16,8},{24,0},{1,25},{9,17},{17,9},{25,1},{2,26},{10... | collective-permute-start | bytes 786440 | tf_op jit(solution)/shard_map/ppermute | solution.py:261
  4.6 12.1 %collective-permute-start.1 = (bf16[512,256]{1,0:T(8,128)(2,1)}, bf16[512,256]{1,0:T(8,128)(2,1)S(1)}, u32[]{:S(2)}, u32[]{:S(2)}) collective-permute-start(bf16[512,256]{1,0:T(8,128)(2,1)} %param.16), channel_id=1, source_target_pairs={{0,16},{8,24},{16,0},{24,8},{1,17},{9,25},{17,1},{25,9},{2,18},{10... | collective-permute-start | bytes 786440 | tf_op jit(solution)/shard_map/ppermute | solution.py:261
  5.1 11.9 %collective-permute-start.2 = (bf16[512,256]{1,0:T(8,128)(2,1)}, bf16[512,256]{1,0:T(8,128)(2,1)S(1)}, u32[]{:S(2)}, u32[]{:S(2)}) collective-permute-start(bf16[512,256]{1,0:T(8,128)(2,1)} %param.16), channel_id=1, source_target_pairs={{0,8},{8,0},{16,24},{24,16},{1,9},{9,1},{17,25},{25,17},{2,10},{10... | collective-permute-start | bytes 786440 | tf_op jit(solution)/shard_map/ppermute | solution.py:261
  18.5 2.9 %collective-permute-start.3 = (bf16[512,256]{1,0:T(8,128)(2,1)S(1)}, bf16[512,256]{1,0:T(8,128)(2,1)S(1)}, u32[]{:S(2)}, u32[]{:S(2)}) collective-permute-start(bf16[512,256]{1,0:T(8,128)(2,1)S(1)} %fusion.34), channel_id=1, source_target_pairs={{0,1},{1,0},{2,3},{3,2},{4,5},{5,4},{6,7},{7,6},{8,9},{9,8},{10,11... | collective-permute-start | bytes 786440 | tf_op jit(solution)/shard_map/ppermute | solution.py:261
  18.5 1.9 %collective-permute-start.5 = (bf16[512,256]{1,0:T(8,128)(2,1)S(1)}, bf16[512,256]{1,0:T(8,128)(2,1)S(1)}, u32[]{:S(2)}, u32[]{:S(2)}) collective-permute-start(bf16[512,256]{1,0:T(8,128)(2,1)S(1)} %fusion.37), channel_id=1, source_target_pairs={{0,1},{1,0},{2,3},{3,2},{4,5},{5,4},{6,7},{7,6},{8,9},{9,8},{10,11... | collective-permute-start | bytes 786440 | tf_op jit(solution)/shard_map/ppermute | solution.py:261
  21.2 15.1 %collective-permute-start.6 = (bf16[512,256]{1,0:T(8,128)(2,1)S(1)}, bf16[512,256]{1,0:T(8,128)(2,1)S(1)}, u32[]{:S(2)}, u32[]{:S(2)}) collective-permute-start(bf16[512,256]{1,0:T(8,128)(2,1)S(1)} %fusion.40), channel_id=1, source_target_pairs={{0,1},{1,0},{2,3},{3,2},{4,5},{5,4},{6,7},{7,6},{8,9},{9,8},{10,11... | collective-permute-start | bytes 786440 | tf_op jit(solution)/shard_map/ppermute | solution.py:261
  21.4 26.4 %copy-start = (bf16[512,256]{1,0:T(8,128)(2,1)S(1)}, bf16[512,256]{1,0:T(8,128)(2,1)}, u32[]{:S(2)}) copy-start(bf16[512,256]{1,0:T(8,128)(2,1)} %refs_6_.1) | copy-start | bytes 786436
  21.4 26.4 %copy-start.1 = (bf16[256,256]{1,0:T(8,128)(2,1)S(1)}, bf16[256,256]{1,0:T(8,128)(2,1)}, u32[]{:S(2)}) copy-start(bf16[256,256]{1,0:T(8,128)(2,1)} %refs_4_.1) | copy-start | bytes 393220
  21.4 26.4 %copy-start.2 = (f32[256]{0:T(256)S(1)}, f32[256]{0:T(256)}, u32[]{:S(2)}) copy-start(f32[256]{0:T(256)} %param.18) | copy-start | bytes 3076
  21.5 8.6 %collective-permute-start.4 = (bf16[512,256]{1,0:T(8,128)(2,1)S(1)}, bf16[512,256]{1,0:T(8,128)(2,1)S(1)}, u32[]{:S(2)}, u32[]{:S(2)}) collective-permute-start(bf16[512,256]{1,0:T(8,128)(2,1)S(1)} %add_convert_fusion), channel_id=1, source_target_pairs={{0,2},{1,3},{2,0},{3,1},{4,6},{5,7},{6,4},{7,5},{8,10},{9,11},{10,... | collective-permute-start | bytes 786440 | tf_op jit(solution)/shard_map/ppermute | solution.py:261
  23.8 9.9 %collective-permute-start.7 = (bf16[512,256]{1,0:T(8,128)(2,1)S(1)}, bf16[512,256]{1,0:T(8,128)(2,1)S(1)}, u32[]{:S(2)}, u32[]{:S(2)}) collective-permute-start(bf16[512,256]{1,0:T(8,128)(2,1)S(1)} %fusion.43), channel_id=1, source_target_pairs={{0,1},{1,0},{2,3},{3,2},{4,5},{5,4},{6,7},{7,6},{8,9},{9,8},{10,11... | collective-permute-start | bytes 786440 | tf_op jit(solution)/shard_map/ppermute | solution.py:261
  24.0 13.0 %collective-permute-start.10 = (bf16[512,256]{1,0:T(8,128)(2,1)S(1)}, bf16[512,256]{1,0:T(8,128)(2,1)S(1)}, u32[]{:S(2)}, u32[]{:S(2)}) collective-permute-start(bf16[512,256]{1,0:T(8,128)(2,1)S(1)} %add_convert_fusion), channel_id=1, source_target_pairs={{2,4},{3,5},{4,2},{5,3},{10,12},{11,13},{12,10},{13,11},{18,20},{1... | collective-permute-start | bytes 786440 | tf_op jit(solution)/shard_map/ppermute | solution.py:266
  30.8 17.0 %collective-permute-start.9 = (bf16[512,256]{1,0:T(8,128)(2,1)S(1)}, bf16[512,256]{1,0:T(8,128)(2,1)S(1)}, u32[]{:S(2)}, u32[]{:S(2)}) collective-permute-start(bf16[512,256]{1,0:T(8,128)(2,1)S(1)} %fusion.31), channel_id=1, source_target_pairs={{0,4},{1,5},{2,6},{3,7},{4,0},{5,1},{6,2},{7,3},{8,12},{9,13},{10,... | collective-permute-start | bytes 786440 | tf_op jit(solution)/shard_map/ppermute | solution.py:261
  34.5 13.4 %collective-permute-start.8 = (bf16[512,256]{1,0:T(8,128)(2,1)S(1)}, bf16[512,256]{1,0:T(8,128)(2,1)S(1)}, u32[]{:S(2)}, u32[]{:S(2)}) collective-permute-start(bf16[512,256]{1,0:T(8,128)(2,1)S(1)} %fusion.28), channel_id=1, source_target_pairs={{0,2},{1,3},{2,0},{3,1},{4,6},{5,7},{6,4},{7,5},{8,10},{9,11},{10,... | collective-permute-start | bytes 786440 | tf_op jit(solution)/shard_map/ppermute | solution.py:261
  49.0 13.7 %collective-permute-start.11 = (bf16[256,512]{1,0:T(8,128)(2,1)S(1)}, bf16[256,512]{1,0:T(8,128)(2,1)S(1)}, u32[]{:S(2)}, u32[]{:S(2)}) collective-permute-start(bf16[256,512]{1,0:T(8,128)(2,1)S(1)} %get-tuple-element.84.refs_1_), channel_id=1, source_target_pairs={{0,4},{1,5},{2,6},{3,7},{4,0},{5,1},{6,2},{7,3},{8,12},{9,13},{10,... | collective-permute-start | bytes 786440 | tf_op jit(solution)/shard_map/ppermute | solution.py:261
  49.0 5.1 %collective-permute-start.12 = (bf16[272,256]{1,0:T(8,128)(2,1)S(1)}, bf16[272,256]{1,0:T(8,128)(2,1)S(1)}, u32[]{:S(2)}, u32[]{:S(2)}) collective-permute-start(bf16[272,256]{1,0:T(8,128)(2,1)S(1)} %get-tuple-element.81), channel_id=1, source_target_pairs={{0,8},{8,0},{16,24},{24,16},{1,9},{9,1},{17,25},{25,17},{2,10},{10... | collective-permute-start | bytes 417800 | tf_op jit(solution)/shard_map/ppermute | solution.py:261
  50.0 13.5 %collective-permute-start.17 = (bf16[256,512]{1,0:T(8,128)(2,1)S(1)}, bf16[256,512]{1,0:T(8,128)(2,1)S(1)}, u32[]{:S(2)}, u32[]{:S(2)}) collective-permute-start(bf16[256,512]{1,0:T(8,128)(2,1)S(1)} %get-tuple-element.84.refs_1_), channel_id=1, source_target_pairs={{0,2},{1,3},{2,0},{3,1},{4,6},{5,7},{6,4},{7,5},{8,10},{9,11},{10,... | collective-permute-start | bytes 786440 | tf_op jit(solution)/shard_map/ppermute | solution.py:261
  52.4 19.2 %collective-permute-start.16 = (bf16[256,512]{1,0:T(8,128)(2,1)S(1)}, bf16[256,512]{1,0:T(8,128)(2,1)S(1)}, u32[]{:S(2)}, u32[]{:S(2)}) collective-permute-start(bf16[256,512]{1,0:T(8,128)(2,1)S(1)} %get-tuple-element.84.refs_1_), channel_id=1, source_target_pairs={{0,1},{1,0},{2,3},{3,2},{4,5},{5,4},{6,7},{7,6},{8,9},{9,8},{10,11... | collective-permute-start | bytes 786440 | tf_op jit(solution)/shard_map/ppermute | solution.py:261
  54.0 14.9 %collective-permute-start.14 = (bf16[256,512]{1,0:T(8,128)(2,1)S(1)}, bf16[256,512]{1,0:T(8,128)(2,1)S(1)}, u32[]{:S(2)}, u32[]{:S(2)}) collective-permute-start(bf16[256,512]{1,0:T(8,128)(2,1)S(1)} %get-tuple-element.84.refs_1_), channel_id=1, source_target_pairs={{2,4},{3,5},{4,2},{5,3},{10,12},{11,13},{12,10},{13,11},{18,20},{1... | collective-permute-start | bytes 786440 | tf_op jit(solution)/shard_map/ppermute | solution.py:266
  62.7 8.9 %collective-permute-start.19 = (bf16[256,512]{1,0:T(8,128)(2,1)S(1)}, bf16[256,512]{1,0:T(8,128)(2,1)S(1)}, u32[]{:S(2)}, u32[]{:S(2)}) collective-permute-start(bf16[256,512]{1,0:T(8,128)(2,1)S(1)} %collective-permute-done.11.refs_3_), channel_id=1, source_target_pairs={{0,1},{1,0},{2,3},{3,2},{4,5},{5,4},{6,7},{7,6},{8,9},{9,8},{10,11... | collective-permute-start | bytes 786440 | tf_op jit(solution)/shard_map/ppermute | solution.py:261
  62.7 8.7 %collective-permute-start.13 = (bf16[256,512]{1,0:T(8,128)(2,1)S(1)}, bf16[256,512]{1,0:T(8,128)(2,1)S(1)}, u32[]{:S(2)}, u32[]{:S(2)}) collective-permute-start(bf16[256,512]{1,0:T(8,128)(2,1)S(1)} %collective-permute-done.11.refs_3_), channel_id=1, source_target_pairs={{0,2},{1,3},{2,0},{3,1},{4,6},{5,7},{6,4},{7,5},{8,10},{9,11},{10,... | collective-permute-start | bytes 786440 | tf_op jit(solution)/shard_map/ppermute | solution.py:261
  63.5 5.4 %collective-permute-start.20 = (bf16[272,256]{1,0:T(8,128)(2,1)S(1)}, bf16[272,256]{1,0:T(8,128)(2,1)S(1)}, u32[]{:S(2)}, u32[]{:S(2)}) collective-permute-start(bf16[272,256]{1,0:T(8,128)(2,1)S(1)} %add_convert_fusion.4), channel_id=1, source_target_pairs={{0,16},{8,24},{16,0},{24,8},{1,17},{9,25},{17,1},{25,9},{2,18},{10... | collective-permute-start | bytes 417800 | tf_op jit(solution)/shard_map/ppermute | solution.py:261
  68.9 2.6 %collective-permute-start.18 = (bf16[256,512]{1,0:T(8,128)(2,1)S(1)}, bf16[256,512]{1,0:T(8,128)(2,1)S(1)}, u32[]{:S(2)}, u32[]{:S(2)}) collective-permute-start(bf16[256,512]{1,0:T(8,128)(2,1)S(1)} %collective-permute-done.17.refs_2_), channel_id=1, source_target_pairs={{0,1},{1,0},{2,3},{3,2},{4,5},{5,4},{6,7},{7,6},{8,9},{9,8},{10,11... | collective-permute-start | bytes 786440 | tf_op jit(solution)/shard_map/ppermute | solution.py:261
  69.0 4.4 %collective-permute-start.21 = (bf16[272,256]{1,0:T(8,128)(2,1)S(1)}, bf16[272,256]{1,0:T(8,128)(2,1)S(1)}, u32[]{:S(2)}, u32[]{:S(2)}) collective-permute-start(bf16[272,256]{1,0:T(8,128)(2,1)S(1)} %add_convert_fusion.3), channel_id=1, source_target_pairs={{0,1},{1,0},{2,3},{3,2},{4,5},{5,4},{6,7},{7,6},{8,9},{9,8},{10,11... | collective-permute-start | bytes 417800 | tf_op jit(solution)/shard_map/ppermute | solution.py:261
  71.5 2.0 %collective-permute-start.15 = (bf16[256,512]{1,0:T(8,128)(2,1)S(1)}, bf16[256,512]{1,0:T(8,128)(2,1)S(1)}, u32[]{:S(2)}, u32[]{:S(2)}) collective-permute-start(bf16[256,512]{1,0:T(8,128)(2,1)S(1)} %broadcast_select_fusion.refs_1_), channel_id=1, source_target_pairs={{0,1},{1,0},{2,3},{3,2},{4,5},{5,4},{6,7},{7,6},{8,9},{9,8},{10,11... | collective-permute-start | bytes 786440 | tf_op jit(solution)/shard_map/ppermute | solution.py:261
  74.0 6.1 %collective-permute-start.25 = (bf16[272,256]{1,0:T(8,128)(2,1)S(1)}, bf16[272,256]{1,0:T(8,128)(2,1)S(1)}, u32[]{:S(2)}, u32[]{:S(2)}) collective-permute-start(bf16[272,256]{1,0:T(8,128)(2,1)S(1)} %add_convert_fusion.2), channel_id=1, source_target_pairs={{0,2},{1,3},{2,0},{3,1},{4,6},{5,7},{6,4},{7,5},{8,10},{9,11},{10,... | collective-permute-start | bytes 417800 | tf_op jit(solution)/shard_map/ppermute | solution.py:261
  74.7 10.1 %collective-permute-start.22 = (bf16[512,256]{1,0:T(8,128)(2,1)S(1)}, bf16[512,256]{1,0:T(8,128)(2,1)S(1)}, u32[]{:S(2)}, u32[]{:S(2)}) collective-permute-start(bf16[512,256]{1,0:T(8,128)(2,1)S(1)} %back_last.3), channel_id=1, source_target_pairs={{0,24},{8,16},{16,8},{24,0},{1,25},{9,17},{17,9},{25,1},{2,26},{10... | collective-permute-start | bytes 786440 | tf_op jit(solution)/shard_map/ppermute | solution.py:261
  76.6 12.2 %collective-permute-start.23 = (bf16[512,256]{1,0:T(8,128)(2,1)S(1)}, bf16[512,256]{1,0:T(8,128)(2,1)S(1)}, u32[]{:S(2)}, u32[]{:S(2)}) collective-permute-start(bf16[512,256]{1,0:T(8,128)(2,1)S(1)} %get-tuple-element.90), channel_id=1, source_target_pairs={{0,8},{8,0},{16,24},{24,16},{1,9},{9,1},{17,25},{25,17},{2,10},{10... | collective-permute-start | bytes 786440 | tf_op jit(solution)/shard_map/ppermute | solution.py:261
  77.9 11.4 %collective-permute-start.24 = (bf16[512,256]{1,0:T(8,128)(2,1)S(1)}, bf16[512,256]{1,0:T(8,128)(2,1)S(1)}, u32[]{:S(2)}, u32[]{:S(2)}) collective-permute-start(bf16[512,256]{1,0:T(8,128)(2,1)S(1)} %get-tuple-element.91), channel_id=1, source_target_pairs={{0,16},{8,24},{16,0},{24,8},{1,17},{9,25},{17,1},{25,9},{2,18},{10... | collective-permute-start | bytes 786440 | tf_op jit(solution)/shard_map/ppermute | solution.py:261
  80.1 9.3 %collective-permute-start.26 = (bf16[272,256]{1,0:T(8,128)(2,1)S(1)}, bf16[272,256]{1,0:T(8,128)(2,1)S(1)}, u32[]{:S(2)}, u32[]{:S(2)}) collective-permute-start(bf16[272,256]{1,0:T(8,128)(2,1)S(1)} %add_convert_fusion.1.refs_1_), channel_id=1, source_target_pairs={{0,4},{1,5},{2,6},{3,7},{4,0},{5,1},{6,2},{7,3},{8,12},{9,13},{10,... | collective-permute-start | bytes 417800 | tf_op jit(solution)/shard_map/ppermute | solution.py:261

commit v4 on v2

--- a/solution.py
+++ b/solution.py
@@ -271,13 +271,14 @@
         count = lax.axis_size("col") // 2
         parts = [swap(chunk(k, far).astype(BF16), "col", 2 * k) for k in range(1, count - 1)]
         return [*parts, swap(far, "col", 2 * (count - 1))], chunk(0, far)
-    passed = jnp.where(at_end(), 0.0, swap(far, "col", 2).astype(F32))
+    near = chunk(1, far).astype(BF16)
+    landed = swap(jnp.where(at_end(), far, near), "col", 2)
+    passed = jnp.where(at_end(), 0.0, landed.astype(F32))
     later, ready = lax.optimization_barrier((far, ready))
     middle = move(later, [(1, 2), (2, 1)])
-    both = (chunk(2, passed) + passed).astype(BF16)
-    across = swap(both, "col", 4)
-    near = swap(chunk(1, both).astype(BF16), "col", 2)
-    return [near, across, middle], chunk(0, both)
+    across = swap((chunk(2, passed) + passed).astype(BF16), "col", 4)
+    near = move(near, [(0, 1), (3, 2)])
+    return [jnp.where(at_end(), landed, near), across, middle], chunk(0, far)
 
 
 def gather_far(value, count, hold):

time: 90.5 us -> 90.9 us (level)
  waiting for transfers between devices: 44.5 us -> 38.6 us
  starting transfers between devices: 22.8 us -> 27.5 us
  Pallas kernels: 14.3 us -> 16 us
    ppermute x25 -> x24, waiting for transfers between devices: 44.5 us -> 35.1 us  [swap(): return lax.ppermute(value, axis, [(i, i ^ mask) for i in range(count)])]
    ppermute x2 -> x3, starting transfers between devices: 1.51 us -> 7.83 us  [move(): return lax.ppermute(value, 'col', pairs)]
    ppermute x2 -> x3, waiting for transfers between devices: 0.01 us -> 3.56 us  [move(): return lax.ppermute(value, 'col', pairs)]
    pallas_call x1, Pallas kernels: 6.94 us -> 8.61 us  [densify(): pl.pallas_call(lambda *refs: densify_kernel(per, col_count // 2, bands ==...]
    ppermute x25 -> x24, starting transfers between devices: 21.3 us -> 19.7 us  [swap(): return lax.ppermute(value, axis, [(i, i ^ mask) for i in range(count)])]
  transfers between devices with their start and end apart: 27 -> 27, of which waited for: 14 -> 13; matrix products, arithmetic and copies ran while one was open for 6% -> 6% of each run, Pallas kernels for 13% -> 15%
where the time goes in v4:
time: 90.9 us
  waiting for transfers between devices  38.6 us (42%)
  starting transfers between devices  27.5 us (30%)
  Pallas kernels  16 us (18%)
  matrix products  5.68 us (6%)
  between operations  1.64 us (2%)
  local copies, waits for them, and re-layouts  1.09 us (1%)
    ppermute x24, waiting for transfers between devices, swap(): return lax.ppermute(value, axis, [(i, i ^ mask) for i in range(count)])  35.1 us
    ppermute x24, starting transfers between devices, swap(): return lax.ppermute(value, axis, [(i, i ^ mask) for i in range(count)])  19.7 us
    pallas_call x1, Pallas kernels, densify(): pl.pallas_call(lambda *refs: densify_kernel(per, col_count // 2, bands ==...  8.61 us
    ppermute x3, starting transfers between devices, move(): return lax.ppermute(value, 'col', pairs)  7.83 us
    dot_general x8, matrix products, cell_product(): return jnp.dot(cell_rows(core, k), source, preferred_element_type=F32)  5.68 us
    pallas_call x5, Pallas kernels, back(): pl.pallas_call(lambda *refs: back_kernel(panels, chosen, last, total is n...  5.43 us
    ppermute x3, waiting for transfers between devices, move(): return lax.ppermute(value, 'col', pairs)  3.56 us
  transfers between devices with their start and end apart: 27, of which 13 were waited for; matrix products, arithmetic and copies ran while one was open for 6% of the time, Pallas kernels for 15%

profile of v4, /device:TPU:0, one launch (start us, length us, event | category | flops | bytes accessed | tf_op | source)
XLA Modules:
  0.0 90.9 jit_solution(349291338905833459)
XLA Ops:
  0.6 4.0 %collective-permute-start = (bf16[512,256]{1,0:T(8,128)(2,1)}, bf16[512,256]{1,0:T(8,128)(2,1)S(1)}, u32[]{:S(2)}, u32[]{:S(2)}) collective-permute-start(bf16[512,256]{1,0:T(8,128)(2,1)} %param.16), channel_id=1, source_target_pairs={{0,24},{8,16},{16,8},{24,0},{1,25},{9,17},{17,9},{25,1},{2,26},{10... | collective-permute-start | bytes 786440 | tf_op jit(solution)/shard_map/ppermute | solution.py:261
  4.6 0.5 collective-permute-start.1
  5.9 1.0 %scatter.14 = bf16[2048,256]{1,0:T(8,128)(2,1)S(1)} pad(bf16[512,256]{1,0:T(8,128)(2,1)} %param.16, bf16[]{:T(256)} %constant.131.clone.1), padding=0_1536x0_0 | pad | bytes 1310722 | tf_op jit(solution)/shard_map/scatter | solution.py:318
  6.9 8.6 %densify.1.refs_0_ = bf16[4096,2048]{1,0:T(8,128)(2,1)S(1)} custom-call(s32[1,1,384]{2,1,0:T(1,128)} %refs_0_.1, s32[1,1,384]{2,1,0:T(1,128)} %refs_1_.1, s32[1,1]{1,0:T(1,128)S(6)} %copy.15.refs_2_, bf16[384,128,128]{2,1,0:T(8,128)(2,1)} %bitcast.12, bf16[384,128,128]{2,1,0:T(8,128)(2,1)} %bitcast.13, bf16[384,128,128]{2,1,0:T(8,128)(2,1)} %bitcast.14), custom_call_target="tpu_custom_call" | custom-call | bytes 33554432 | tf_op jit(solution)/shard_map/densify/pallas_call | solution.py:93
  15.6 1.2 %collective-permute-done.1 = bf16[512,256]{1,0:T(8,128)(2,1)S(1)} collective-permute-done((bf16[512,256]{1,0:T(8,128)(2,1)}, bf16[512,256]{1,0:T(8,128)(2,1)S(1)}, u32[]{:S(2)}, u32[]{:S(2)}) %collective-permute-start.1) | collective-permute-done | bytes 262176 | tf_op jit(solution)/shard_map/ppermute | solution.py:261
  16.7 0.3 collective-permute-done.2
  17.0 0.7 fusion.40
  17.8 0.7 fusion.34
  18.5 0.6 collective-permute-start.3
  19.1 0.2 collective-permute-done.4
  19.4 0.7 fusion.43
  20.1 0.2 collective-permute-start.6
  20.3 0.7 fusion.12
  21.1 0.6 collective-permute-done.6
  21.7 0.7 broadcast_select_fusion.2
  22.4 1.6 %collective-permute-start.7 = (bf16[512,256]{1,0:T(8,128)(2,1)S(1)}, bf16[512,256]{1,0:T(8,128)(2,1)S(1)}, u32[]{:S(2)}, u32[]{:S(2)}) collective-permute-start(bf16[512,256]{1,0:T(8,128)(2,1)S(1)} %get-tuple-element.92), channel_id=1, source_target_pairs={{0,2},{1,3},{2,0},{3,1},{4,6},{5,7},{6,4},{7,5},{8,10},{9,11},{10,... | collective-permute-start | bytes 786440 | tf_op jit(solution)/shard_map/ppermute | solution.py:261
  24.0 0.7 fusion.37
  24.8 0.7 collective-permute-start.10
  25.5 6.3 %collective-permute-start.8 = (bf16[512,256]{1,0:T(8,128)(2,1)S(1)}, bf16[512,256]{1,0:T(8,128)(2,1)S(1)}, u32[]{:S(2)}, u32[]{:S(2)}) collective-permute-start(bf16[512,256]{1,0:T(8,128)(2,1)S(1)} %get-tuple-element.93), channel_id=1, source_target_pairs={{0,2},{1,3},{6,4},{7,5},{8,10},{9,11},{14,12},{15,13},{16,18},{17,... | collective-permute-start | bytes 786440 | tf_op jit(solution)/shard_map/ppermute | solution.py:266
  31.8 0.7 fusion.28
  32.5 1.6 %collective-permute-start.9 = (bf16[512,256]{1,0:T(8,128)(2,1)S(1)}, bf16[512,256]{1,0:T(8,128)(2,1)S(1)}, u32[]{:S(2)}, u32[]{:S(2)}) collective-permute-start(bf16[512,256]{1,0:T(8,128)(2,1)S(1)} %fusion.28), channel_id=1, source_target_pairs={{0,4},{1,5},{2,6},{3,7},{4,0},{5,1},{6,2},{7,3},{8,12},{9,13},{10,... | collective-permute-start | bytes 786440 | tf_op jit(solution)/shard_map/ppermute | solution.py:261
  34.2 0.7 fusion.16.refs_0_
  34.9 3.6 %collective-permute-done.8 = bf16[512,256]{1,0:T(8,128)(2,1)S(1)} collective-permute-done((bf16[512,256]{1,0:T(8,128)(2,1)S(1)}, bf16[512,256]{1,0:T(8,128)(2,1)S(1)}, u32[]{:S(2)}, u32[]{:S(2)}) %collective-permute-start.8) | collective-permute-done | bytes 262176 | tf_op jit(solution)/shard_map/ppermute | solution.py:266
  38.5 9.0 %collective-permute-done.9.refs_2_ = bf16[512,256]{1,0:T(8,128)(2,1)S(1)} collective-permute-done((bf16[512,256]{1,0:T(8,128)(2,1)S(1)}, bf16[512,256]{1,0:T(8,128)(2,1)S(1)}, u32[]{:S(2)}, u32[]{:S(2)}) %collective-permute-start.9) | collective-permute-done | bytes 262176 | tf_op jit(solution)/shard_map/ppermute | solution.py:261
  47.5 1.1 %dense.1 = (bf16[512,256]{1,0:T(8,128)(2,1)}, bf16[256,512]{1,0:T(8,128)(2,1)S(1)}, bf16[272,256]{1,0:T(8,128)(2,1)S(1)}) custom-call(f32[512,256]{1,0:T(8,128)S(1)} %fusion.16.refs_0_, bf16[512,256]{1,0:T(8,128)(2,1)S(1)} %broadcast_select_fusion.1.refs_1_, bf16[512,256]{1,0:T(8,128)(2,1)S(1)} %collective-permute-done.9.refs_2_, ...), custom_call_target="tpu_custom_call" | custom-call | flops 201326592 | bytes 1048576 | tf_op jit(solution)/shard_map/dense/pallas_call | solution.py:157
  48.6 1.5 %collective-permute-start.12 = (bf16[272,256]{1,0:T(8,128)(2,1)S(1)}, bf16[272,256]{1,0:T(8,128)(2,1)S(1)}, u32[]{:S(2)}, u32[]{:S(2)}) collective-permute-start(bf16[272,256]{1,0:T(8,128)(2,1)S(1)} %get-tuple-element.79), channel_id=1, source_target_pairs={{0,8},{8,0},{16,24},{24,16},{1,9},{9,1},{17,25},{25,17},{2,10},{10... | collective-permute-start | bytes 417800 | tf_op jit(solution)/shard_map/ppermute | solution.py:261
  50.1 3.2 %collective-permute-start.17 = (bf16[256,512]{1,0:T(8,128)(2,1)S(1)}, bf16[256,512]{1,0:T(8,128)(2,1)S(1)}, u32[]{:S(2)}, u32[]{:S(2)}) collective-permute-start(bf16[256,512]{1,0:T(8,128)(2,1)S(1)} %get-tuple-element.78.refs_1_), channel_id=1, source_target_pairs={{0,2},{1,3},{2,0},{3,1},{4,6},{5,7},{6,4},{7,5},{8,10},{9,11},{10,... | collective-permute-start | bytes 786440 | tf_op jit(solution)/shard_map/ppermute | solution.py:261
  53.3 0.8 collective-permute-start.14
  54.2 8.6 %collective-permute-done.11.refs_3_ = bf16[256,512]{1,0:T(8,128)(2,1)S(1)} collective-permute-done((bf16[256,512]{1,0:T(8,128)(2,1)S(1)}, bf16[256,512]{1,0:T(8,128)(2,1)S(1)}, u32[]{:S(2)}, u32[]{:S(2)}) %collective-permute-start.11) | collective-permute-done | bytes 262176 | tf_op jit(solution)/shard_map/ppermute | solution.py:261
  62.8 1.2 %collective-permute-done.17.refs_2_ = bf16[256,512]{1,0:T(8,128)(2,1)S(1)} collective-permute-done((bf16[256,512]{1,0:T(8,128)(2,1)S(1)}, bf16[256,512]{1,0:T(8,128)(2,1)S(1)}, u32[]{:S(2)}, u32[]{:S(2)}) %collective-permute-start.17) | collective-permute-done | bytes 262176 | tf_op jit(solution)/shard_map/ppermute | solution.py:261
  64.0 0.9 collective-permute-start.20
  64.9 1.8 %back.2.refs_4_ = f32[256,2048]{1,0:T(8,128)S(1)} custom-call(bf16[4096,2048]{1,0:T(8,128)(2,1)S(1)} %densify.1.refs_0_, bf16[256,512]{1,0:T(8,128)(2,1)S(1)} %get-tuple-element.78.refs_1_, bf16[256,512]{1,0:T(8,128)(2,1)S(1)} %collective-permute-done.17.refs_2_, bf16[256,512]{1,0:T(8,128)(2,1)S(1)} %collective-permute-done.11.refs_3_), custom_call_target="tpu_custom_call" | custom-call | flops 1610612736 | bytes 3145728 | tf_op jit(solution)/shard_map/back/pallas_call | solution.py:218
  66.6 2.6 %collective-permute-done.20 = bf16[272,256]{1,0:T(8,128)(2,1)S(1)} collective-permute-done((bf16[272,256]{1,0:T(8,128)(2,1)S(1)}, bf16[272,256]{1,0:T(8,128)(2,1)S(1)}, u32[]{:S(2)}, u32[]{:S(2)}) %collective-permute-start.20) | collective-permute-done | bytes 139296 | tf_op jit(solution)/shard_map/ppermute | solution.py:261
  69.3 0.6 collective-permute-start.21
  69.8 1.7 %collective-permute-done.13 = bf16[256,512]{1,0:T(8,128)(2,1)S(1)} collective-permute-done((bf16[256,512]{1,0:T(8,128)(2,1)S(1)}, bf16[256,512]{1,0:T(8,128)(2,1)S(1)}, u32[]{:S(2)}, u32[]{:S(2)}) %collective-permute-start.13) | collective-permute-done | bytes 262176 | tf_op jit(solution)/shard_map/ppermute | solution.py:261
  71.6 1.8 %back.3.refs_3_ = f32[256,2048]{1,0:T(8,128)S(1)} custom-call(bf16[4096,2048]{1,0:T(8,128)(2,1)S(1)} %densify.1.refs_0_, bf16[256,512]{1,0:T(8,128)(2,1)S(1)} %collective-permute-done.16.refs_1_, bf16[256,512]{1,0:T(8,128)(2,1)S(1)} %collective-permute-done.18.refs_2_, bf16[256,512]{1,0:T(8,128)(2,1)S(1)} %collective-permute-done.19.refs_3_, ...), custom_call_target="tpu_custom_call" | custom-call | flops 1610612736 | bytes 3145728 | tf_op jit(solution)/shard_map/back/pallas_call | solution.py:218
  73.5 0.5 back_last.3
  74.0 0.9 collective-permute-start.25
  74.9 1.5 %collective-permute-start.22 = (bf16[512,256]{1,0:T(8,128)(2,1)S(1)}, bf16[512,256]{1,0:T(8,128)(2,1)S(1)}, u32[]{:S(2)}, u32[]{:S(2)}) collective-permute-start(bf16[512,256]{1,0:T(8,128)(2,1)S(1)} %back_last.3), channel_id=1, source_target_pairs={{0,24},{8,16},{16,8},{24,0},{1,25},{9,17},{17,9},{25,1},{2,26},{10... | collective-permute-start | bytes 786440 | tf_op jit(solution)/shard_map/ppermute | solution.py:261
  76.4 0.8 back_last.5
  77.2 1.8 %collective-permute-start.23 = (bf16[512,256]{1,0:T(8,128)(2,1)S(1)}, bf16[512,256]{1,0:T(8,128)(2,1)S(1)}, u32[]{:S(2)}, u32[]{:S(2)}) collective-permute-start(bf16[512,256]{1,0:T(8,128)(2,1)S(1)} %get-tuple-element.86), channel_id=1, source_target_pairs={{0,8},{8,0},{16,24},{24,16},{1,9},{9,1},{17,25},{25,17},{2,10},{10... | collective-permute-start | bytes 786440 | tf_op jit(solution)/shard_map/ppermute | solution.py:261
  79.0 0.3 collective-permute-start.24
  79.3 0.9 collective-permute-done.25
  80.2 0.2 collective-permute-start.26
  80.4 4.6 %collective-permute-done.22 = bf16[512,256]{1,0:T(8,128)(2,1)S(1)} collective-permute-done((bf16[512,256]{1,0:T(8,128)(2,1)S(1)}, bf16[512,256]{1,0:T(8,128)(2,1)S(1)}, u32[]{:S(2)}, u32[]{:S(2)}) %collective-permute-start.22) | collective-permute-done | bytes 262176 | tf_op jit(solution)/shard_map/ppermute | solution.py:261
  85.1 0.6 back_last.4
  85.6 4.3 %collective-permute-done.23 = bf16[512,256]{1,0:T(8,128)(2,1)S(1)} collective-permute-done((bf16[512,256]{1,0:T(8,128)(2,1)S(1)}, bf16[512,256]{1,0:T(8,128)(2,1)S(1)}, u32[]{:S(2)}, u32[]{:S(2)}) %collective-permute-start.23) | collective-permute-done | bytes 262176 | tf_op jit(solution)/shard_map/ppermute | solution.py:261
  90.0 0.8 finish.1
  (40 shorter events, 0.8 us)
Async XLA Ops:
  0.6 14.9 %collective-permute-start = (bf16[512,256]{1,0:T(8,128)(2,1)}, bf16[512,256]{1,0:T(8,128)(2,1)S(1)}, u32[]{:S(2)}, u32[]{:S(2)}) collective-permute-start(bf16[512,256]{1,0:T(8,128)(2,1)} %param.16), channel_id=1, source_target_pairs={{0,24},{8,16},{16,8},{24,0},{1,25},{9,17},{17,9},{25,1},{2,26},{10... | collective-permute-start | bytes 786440 | tf_op jit(solution)/shard_map/ppermute | solution.py:261
  4.6 12.1 %collective-permute-start.1 = (bf16[512,256]{1,0:T(8,128)(2,1)}, bf16[512,256]{1,0:T(8,128)(2,1)S(1)}, u32[]{:S(2)}, u32[]{:S(2)}) collective-permute-start(bf16[512,256]{1,0:T(8,128)(2,1)} %param.16), channel_id=1, source_target_pairs={{0,16},{8,24},{16,0},{24,8},{1,17},{9,25},{17,1},{25,9},{2,18},{10... | collective-permute-start | bytes 786440 | tf_op jit(solution)/shard_map/ppermute | solution.py:261
  5.1 11.9 %collective-permute-start.2 = (bf16[512,256]{1,0:T(8,128)(2,1)}, bf16[512,256]{1,0:T(8,128)(2,1)S(1)}, u32[]{:S(2)}, u32[]{:S(2)}) collective-permute-start(bf16[512,256]{1,0:T(8,128)(2,1)} %param.16), channel_id=1, source_target_pairs={{0,8},{8,0},{16,24},{24,16},{1,9},{9,1},{17,25},{25,17},{2,10},{10... | collective-permute-start | bytes 786440 | tf_op jit(solution)/shard_map/ppermute | solution.py:261
  17.8 1.6 %collective-permute-start.4 = (bf16[512,256]{1,0:T(8,128)(2,1)S(1)}, bf16[512,256]{1,0:T(8,128)(2,1)S(1)}, u32[]{:S(2)}, u32[]{:S(2)}) collective-permute-start(bf16[512,256]{1,0:T(8,128)(2,1)S(1)} %fusion.40), channel_id=1, source_target_pairs={{0,1},{1,0},{2,3},{3,2},{4,5},{5,4},{6,7},{7,6},{8,9},{9,8},{10,11... | collective-permute-start | bytes 786440 | tf_op jit(solution)/shard_map/ppermute | solution.py:261
  18.5 2.4 %collective-permute-start.3 = (bf16[512,256]{1,0:T(8,128)(2,1)S(1)}, bf16[512,256]{1,0:T(8,128)(2,1)S(1)}, u32[]{:S(2)}, u32[]{:S(2)}) collective-permute-start(bf16[512,256]{1,0:T(8,128)(2,1)S(1)} %fusion.34), channel_id=1, source_target_pairs={{0,1},{1,0},{2,3},{3,2},{4,5},{5,4},{6,7},{7,6},{8,9},{9,8},{10,11... | collective-permute-start | bytes 786440 | tf_op jit(solution)/shard_map/ppermute | solution.py:261
  20.1 1.6 %collective-permute-start.6 = (bf16[512,256]{1,0:T(8,128)(2,1)S(1)}, bf16[512,256]{1,0:T(8,128)(2,1)S(1)}, u32[]{:S(2)}, u32[]{:S(2)}) collective-permute-start(bf16[512,256]{1,0:T(8,128)(2,1)S(1)} %fusion.43), channel_id=1, source_target_pairs={{0,1},{1,0},{2,3},{3,2},{4,5},{5,4},{6,7},{7,6},{8,9},{9,8},{10,11... | collective-permute-start | bytes 786440 | tf_op jit(solution)/shard_map/ppermute | solution.py:261
  21.1 26.4 %copy-start = (bf16[512,256]{1,0:T(8,128)(2,1)S(1)}, bf16[512,256]{1,0:T(8,128)(2,1)}, u32[]{:S(2)}) copy-start(bf16[512,256]{1,0:T(8,128)(2,1)} %refs_6_.1) | copy-start | bytes 786436
  21.1 26.4 %copy-start.1 = (bf16[256,256]{1,0:T(8,128)(2,1)S(1)}, bf16[256,256]{1,0:T(8,128)(2,1)}, u32[]{:S(2)}) copy-start(bf16[256,256]{1,0:T(8,128)(2,1)} %refs_4_.1) | copy-start | bytes 393220
  21.1 26.4 %copy-start.2 = (f32[256]{0:T(256)S(1)}, f32[256]{0:T(256)}, u32[]{:S(2)}) copy-start(f32[256]{0:T(256)} %param.18) | copy-start | bytes 3076
  22.4 9.4 %collective-permute-start.7 = (bf16[512,256]{1,0:T(8,128)(2,1)S(1)}, bf16[512,256]{1,0:T(8,128)(2,1)S(1)}, u32[]{:S(2)}, u32[]{:S(2)}) collective-permute-start(bf16[512,256]{1,0:T(8,128)(2,1)S(1)} %get-tuple-element.92), channel_id=1, source_target_pairs={{0,2},{1,3},{2,0},{3,1},{4,6},{5,7},{6,4},{7,5},{8,10},{9,11},{10,... | collective-permute-start | bytes 786440 | tf_op jit(solution)/shard_map/ppermute | solution.py:261
  24.7 9.4 %collective-permute-start.5 = (bf16[512,256]{1,0:T(8,128)(2,1)S(1)}, bf16[512,256]{1,0:T(8,128)(2,1)S(1)}, u32[]{:S(2)}, u32[]{:S(2)}) collective-permute-start(bf16[512,256]{1,0:T(8,128)(2,1)S(1)} %fusion.37), channel_id=1, source_target_pairs={{0,1},{1,0},{2,3},{3,2},{4,5},{5,4},{6,7},{7,6},{8,9},{9,8},{10,11... | collective-permute-start | bytes 786440 | tf_op jit(solution)/shard_map/ppermute | solution.py:261
  24.8 13.7 %collective-permute-start.10 = (bf16[512,256]{1,0:T(8,128)(2,1)S(1)}, bf16[512,256]{1,0:T(8,128)(2,1)S(1)}, u32[]{:S(2)}, u32[]{:S(2)}) collective-permute-start(bf16[512,256]{1,0:T(8,128)(2,1)S(1)} %add_convert_fusion), channel_id=1, source_target_pairs={{2,4},{3,5},{4,2},{5,3},{10,12},{11,13},{12,10},{13,11},{18,20},{1... | collective-permute-start | bytes 786440 | tf_op jit(solution)/shard_map/ppermute | solution.py:266
  25.5 12.9 %collective-permute-start.8 = (bf16[512,256]{1,0:T(8,128)(2,1)S(1)}, bf16[512,256]{1,0:T(8,128)(2,1)S(1)}, u32[]{:S(2)}, u32[]{:S(2)}) collective-permute-start(bf16[512,256]{1,0:T(8,128)(2,1)S(1)} %get-tuple-element.93), channel_id=1, source_target_pairs={{0,2},{1,3},{6,4},{7,5},{8,10},{9,11},{14,12},{15,13},{16,18},{17,... | collective-permute-start | bytes 786440 | tf_op jit(solution)/shard_map/ppermute | solution.py:266
  32.5 15.0 %collective-permute-start.9 = (bf16[512,256]{1,0:T(8,128)(2,1)S(1)}, bf16[512,256]{1,0:T(8,128)(2,1)S(1)}, u32[]{:S(2)}, u32[]{:S(2)}) collective-permute-start(bf16[512,256]{1,0:T(8,128)(2,1)S(1)} %fusion.28), channel_id=1, source_target_pairs={{0,4},{1,5},{2,6},{3,7},{4,0},{5,1},{6,2},{7,3},{8,12},{9,13},{10,... | collective-permute-start | bytes 786440 | tf_op jit(solution)/shard_map/ppermute | solution.py:261
  48.6 14.2 %collective-permute-start.11 = (bf16[256,512]{1,0:T(8,128)(2,1)S(1)}, bf16[256,512]{1,0:T(8,128)(2,1)S(1)}, u32[]{:S(2)}, u32[]{:S(2)}) collective-permute-start(bf16[256,512]{1,0:T(8,128)(2,1)S(1)} %get-tuple-element.78.refs_1_), channel_id=1, source_target_pairs={{0,4},{1,5},{2,6},{3,7},{4,0},{5,1},{6,2},{7,3},{8,12},{9,13},{10,... | collective-permute-start | bytes 786440 | tf_op jit(solution)/shard_map/ppermute | solution.py:261
  48.6 5.6 %collective-permute-start.12 = (bf16[272,256]{1,0:T(8,128)(2,1)S(1)}, bf16[272,256]{1,0:T(8,128)(2,1)S(1)}, u32[]{:S(2)}, u32[]{:S(2)}) collective-permute-start(bf16[272,256]{1,0:T(8,128)(2,1)S(1)} %get-tuple-element.79), channel_id=1, source_target_pairs={{0,8},{8,0},{16,24},{24,16},{1,9},{9,1},{17,25},{25,17},{2,10},{10... | collective-permute-start | bytes 417800 | tf_op jit(solution)/shard_map/ppermute | solution.py:261
  50.1 13.9 %collective-permute-start.17 = (bf16[256,512]{1,0:T(8,128)(2,1)S(1)}, bf16[256,512]{1,0:T(8,128)(2,1)S(1)}, u32[]{:S(2)}, u32[]{:S(2)}) collective-permute-start(bf16[256,512]{1,0:T(8,128)(2,1)S(1)} %get-tuple-element.78.refs_1_), channel_id=1, source_target_pairs={{0,2},{1,3},{2,0},{3,1},{4,6},{5,7},{6,4},{7,5},{8,10},{9,11},{10,... | collective-permute-start | bytes 786440 | tf_op jit(solution)/shard_map/ppermute | solution.py:261
  53.3 18.3 %collective-permute-start.16 = (bf16[256,512]{1,0:T(8,128)(2,1)S(1)}, bf16[256,512]{1,0:T(8,128)(2,1)S(1)}, u32[]{:S(2)}, u32[]{:S(2)}) collective-permute-start(bf16[256,512]{1,0:T(8,128)(2,1)S(1)} %get-tuple-element.78.refs_1_), channel_id=1, source_target_pairs={{0,1},{1,0},{2,3},{3,2},{4,5},{5,4},{6,7},{7,6},{8,9},{9,8},{10,11... | collective-permute-start | bytes 786440 | tf_op jit(solution)/shard_map/ppermute | solution.py:261
  53.3 15.9 %collective-permute-start.14 = (bf16[256,512]{1,0:T(8,128)(2,1)S(1)}, bf16[256,512]{1,0:T(8,128)(2,1)S(1)}, u32[]{:S(2)}, u32[]{:S(2)}) collective-permute-start(bf16[256,512]{1,0:T(8,128)(2,1)S(1)} %get-tuple-element.78.refs_1_), channel_id=1, source_target_pairs={{2,4},{3,5},{4,2},{5,3},{10,12},{11,13},{12,10},{13,11},{18,20},{1... | collective-permute-start | bytes 786440 | tf_op jit(solution)/shard_map/ppermute | solution.py:266
  62.8 8.9 %collective-permute-start.19 = (bf16[256,512]{1,0:T(8,128)(2,1)S(1)}, bf16[256,512]{1,0:T(8,128)(2,1)S(1)}, u32[]{:S(2)}, u32[]{:S(2)}) collective-permute-start(bf16[256,512]{1,0:T(8,128)(2,1)S(1)} %collective-permute-done.11.refs_3_), channel_id=1, source_target_pairs={{0,1},{1,0},{2,3},{3,2},{4,5},{5,4},{6,7},{7,6},{8,9},{9,8},{10,11... | collective-permute-start | bytes 786440 | tf_op jit(solution)/shard_map/ppermute | solution.py:261
  62.8 8.7 %collective-permute-start.13 = (bf16[256,512]{1,0:T(8,128)(2,1)S(1)}, bf16[256,512]{1,0:T(8,128)(2,1)S(1)}, u32[]{:S(2)}, u32[]{:S(2)}) collective-permute-start(bf16[256,512]{1,0:T(8,128)(2,1)S(1)} %collective-permute-done.11.refs_3_), channel_id=1, source_target_pairs={{0,2},{1,3},{2,0},{3,1},{4,6},{5,7},{6,4},{7,5},{8,10},{9,11},{10,... | collective-permute-start | bytes 786440 | tf_op jit(solution)/shard_map/ppermute | solution.py:261
  64.0 5.2 %collective-permute-start.20 = (bf16[272,256]{1,0:T(8,128)(2,1)S(1)}, bf16[272,256]{1,0:T(8,128)(2,1)S(1)}, u32[]{:S(2)}, u32[]{:S(2)}) collective-permute-start(bf16[272,256]{1,0:T(8,128)(2,1)S(1)} %add_convert_fusion.4), channel_id=1, source_target_pairs={{0,16},{8,24},{16,0},{24,8},{1,17},{9,25},{17,1},{25,9},{2,18},{10... | collective-permute-start | bytes 417800 | tf_op jit(solution)/shard_map/ppermute | solution.py:261
  69.2 2.4 %collective-permute-start.18 = (bf16[256,512]{1,0:T(8,128)(2,1)S(1)}, bf16[256,512]{1,0:T(8,128)(2,1)S(1)}, u32[]{:S(2)}, u32[]{:S(2)}) collective-permute-start(bf16[256,512]{1,0:T(8,128)(2,1)S(1)} %collective-permute-done.17.refs_2_), channel_id=1, source_target_pairs={{0,1},{1,0},{2,3},{3,2},{4,5},{5,4},{6,7},{7,6},{8,9},{9,8},{10,11... | collective-permute-start | bytes 786440 | tf_op jit(solution)/shard_map/ppermute | solution.py:261
  69.3 4.2 %collective-permute-start.21 = (bf16[272,256]{1,0:T(8,128)(2,1)S(1)}, bf16[272,256]{1,0:T(8,128)(2,1)S(1)}, u32[]{:S(2)}, u32[]{:S(2)}) collective-permute-start(bf16[272,256]{1,0:T(8,128)(2,1)S(1)} %add_convert_fusion.3), channel_id=1, source_target_pairs={{0,1},{1,0},{2,3},{3,2},{4,5},{5,4},{6,7},{7,6},{8,9},{9,8},{10,11... | collective-permute-start | bytes 417800 | tf_op jit(solution)/shard_map/ppermute | solution.py:261
  71.5 2.0 %collective-permute-start.15 = (bf16[256,512]{1,0:T(8,128)(2,1)S(1)}, bf16[256,512]{1,0:T(8,128)(2,1)S(1)}, u32[]{:S(2)}, u32[]{:S(2)}) collective-permute-start(bf16[256,512]{1,0:T(8,128)(2,1)S(1)} %broadcast_select_fusion.refs_1_), channel_id=1, source_target_pairs={{0,1},{1,0},{2,3},{3,2},{4,5},{5,4},{6,7},{7,6},{8,9},{9,8},{10,11... | collective-permute-start | bytes 786440 | tf_op jit(solution)/shard_map/ppermute | solution.py:261
  74.0 6.1 %collective-permute-start.25 = (bf16[272,256]{1,0:T(8,128)(2,1)S(1)}, bf16[272,256]{1,0:T(8,128)(2,1)S(1)}, u32[]{:S(2)}, u32[]{:S(2)}) collective-permute-start(bf16[272,256]{1,0:T(8,128)(2,1)S(1)} %add_convert_fusion.2), channel_id=1, source_target_pairs={{0,2},{1,3},{2,0},{3,1},{4,6},{5,7},{6,4},{7,5},{8,10},{9,11},{10,... | collective-permute-start | bytes 417800 | tf_op jit(solution)/shard_map/ppermute | solution.py:261
  74.9 10.1 %collective-permute-start.22 = (bf16[512,256]{1,0:T(8,128)(2,1)S(1)}, bf16[512,256]{1,0:T(8,128)(2,1)S(1)}, u32[]{:S(2)}, u32[]{:S(2)}) collective-permute-start(bf16[512,256]{1,0:T(8,128)(2,1)S(1)} %back_last.3), channel_id=1, source_target_pairs={{0,24},{8,16},{16,8},{24,0},{1,25},{9,17},{17,9},{25,1},{2,26},{10... | collective-permute-start | bytes 786440 | tf_op jit(solution)/shard_map/ppermute | solution.py:261
  77.2 12.7 %collective-permute-start.23 = (bf16[512,256]{1,0:T(8,128)(2,1)S(1)}, bf16[512,256]{1,0:T(8,128)(2,1)S(1)}, u32[]{:S(2)}, u32[]{:S(2)}) collective-permute-start(bf16[512,256]{1,0:T(8,128)(2,1)S(1)} %get-tuple-element.86), channel_id=1, source_target_pairs={{0,8},{8,0},{16,24},{24,16},{1,9},{9,1},{17,25},{25,17},{2,10},{10... | collective-permute-start | bytes 786440 | tf_op jit(solution)/shard_map/ppermute | solution.py:261
  79.0 10.9 %collective-permute-start.24 = (bf16[512,256]{1,0:T(8,128)(2,1)S(1)}, bf16[512,256]{1,0:T(8,128)(2,1)S(1)}, u32[]{:S(2)}, u32[]{:S(2)}) collective-permute-start(bf16[512,256]{1,0:T(8,128)(2,1)S(1)} %get-tuple-element.87), channel_id=1, source_target_pairs={{0,16},{8,24},{16,0},{24,8},{1,17},{9,25},{17,1},{25,9},{2,18},{10... | collective-permute-start | bytes 786440 | tf_op jit(solution)/shard_map/ppermute | solution.py:261
  80.2 9.8 %collective-permute-start.26 = (bf16[272,256]{1,0:T(8,128)(2,1)S(1)}, bf16[272,256]{1,0:T(8,128)(2,1)S(1)}, u32[]{:S(2)}, u32[]{:S(2)}) collective-permute-start(bf16[272,256]{1,0:T(8,128)(2,1)S(1)} %add_convert_fusion.1.refs_1_), channel_id=1, source_target_pairs={{0,4},{1,5},{2,6},{3,7},{4,0},{5,1},{6,2},{7,3},{8,12},{9,13},{10,... | collective-permute-start | bytes 417800 | tf_op jit(solution)/shard_map/ppermute | solution.py:261
